TPU v7x, 256 devices: a whole 4x4x8 slice. The times are simulated.
256 devices in a mesh: row: 8 (over y, core), col: 32 (over x, z).
Axes of the slice: x: 4, y: 4, z: 8, core: 2. Of those that a mesh axis runs over, the one named last changes fastest.
Arguments:
- left_factors: bfloat16 [16384, 4096], P('row', 'col'), may hold values from -0.125 to 0.125
- right_factors: bfloat16 [16384, 4096], P('row', 'col'), may hold values from -0.078125 to 0.078125
- closing_left: bfloat16 [2048, 4096], P(None, 'col'), may hold values from -0.125 to 0.125
- closing_right: bfloat16 [2048, 4096], P(None, 'col'), may hold values from -0.078125 to 0.078125
- panel_left: bfloat16 [16384, 128], P('row'), may hold values from -0.125 to 0.125
- panel_right: bfloat16 [16384, 128], P('row'), may hold values from -0.09375 to 0.09375
- diag_inverse: bfloat16 [16384, 2048], P('row'), may hold values from -1 to 2, as said below
- fronts: bfloat16 [16384, 4096], P('row', 'col'), may hold values from -6 to 6
Outputs:
- solved: float32 [16384, 4096], P('row', 'col')
- handoff: float32 [2048, 4096], P('row', 'col')
Inputs may be any that keep to these rules, and one draw needn't show every extreme that they name: Each tile of diag_inverse is lower triangular with its diagonal between 0.5 and 2.
All inputs are finite; a program needn't handle non-finite values.
Results may differ from a plain program's by a relative error of at most 0.0012.
Values may be sent and summed in bfloat16 or wider, within the bound.
No kernel may reach another device: no remote copies, remote signals or barrier semaphores. Data moves between devices by JAX's collectives and lax.ppermute only.
A program may use at most 128 MiB of HBM per device.

v0:
```python
import jax
import jax.numpy as jnp
from jax import lax
from jax.experimental import pallas as pl
from jax.experimental.pallas import tpu as pltpu
from jax.sharding import PartitionSpec as P

SUB = 3
NX, NZ = 4, 8
NOTE = 16

HI = lax.Precision.HIGHEST
f32, bf16, f16 = jnp.float32, jnp.bfloat16, jnp.float16

Z_GROUPS = [[x * NZ + z for z in range(NZ)] for x in range(NX)]
MATE = [(c, c ^ 1) for c in range(NX * NZ)]


def along_x(step):
    return [(c, (c // NZ + step) % NX * NZ + c % NZ) for c in range(NX * NZ)]


def along_z(step):
    return [(c, c // NZ * NZ + (c % NZ + 2 * step) % NZ) for c in range(NX * NZ)]


def across(up, step):
    columns = NX * NZ
    route = []
    for row in range(8):
        if up < 0 or row + up < 8:
            route += [(row * columns + a, (row + up) % 8 * columns + b) for a, b in along_x(step)]
    return route


def from_behind(block, axis, distance):
    devices = range(lax.axis_size(axis))
    route = [(i - distance, i) for i in devices if i - distance in devices]
    return lax.ppermute(block, axis, route)


def total(block, route):
    got = [lax.ppermute(block, "col", route(d)) for d in (2, 1, 3)]
    return (block + got[0]) + (got[1] + got[2])


def in_order(near, place):
    line = jnp.concatenate(near[::-1] + near[:0:-1], 0)
    size = near[0].shape[0]
    return lax.dynamic_slice_in_dim(line, (3 - place) * size, 4 * size, 0)


def inverse_factor_kernel(gram_ref, out_ref):
    size = gram_ref.shape[0]
    tiles = size // 8
    row = lax.broadcasted_iota(jnp.int32, (8, size), 0)
    lane = lax.broadcasted_iota(jnp.int32, (8, size), 1)
    left = [gram_ref[8 * i:8 * i + 8, :] for i in range(tiles)]
    right = [jnp.where(lane == row + 8 * i, 1.0, 0.0) for i in range(tiles)]
    for p in range(tiles):
        columns = [
            [jnp.broadcast_to(left[i][:, 8 * p + j:8 * p + j + 1], (8, size)) for i in range(p, tiles)]
            for j in range(8)
        ]
        scales = jnp.zeros((8, size), f32)
        for j in range(8):
            pivot = columns[j][0][j:j + 1, :]
            over = 1.0 / pivot
            scales = jnp.where(row == j, lax.rsqrt(pivot), scales)
            ratio = [c * over for c in columns[j]]
            for l in range(j + 1, 8):
                times = ratio[0][l:l + 1, :]
                columns[l] = [c - times * d for c, d in zip(columns[l], columns[j])]
            ratio[0] = jnp.where(row > j, ratio[0], 0.0)
            left_row, right_row = left[p][j:j + 1, :], right[p][j:j + 1, :]
            for i in range(p, tiles):
                left[i] = left[i] - ratio[i - p] * left_row
                right[i] = right[i] - ratio[i - p] * right_row
        out_ref[8 * p:8 * p + 8, :] = right[p] * scales


def inverse_factor(both, rank):
    return pl.pallas_call(
        inverse_factor_kernel,
        grid=(1,),
        in_specs=[pl.BlockSpec((rank, rank), lambda i: (both.shape[0] // rank - 1, 0))],
        out_specs=pl.BlockSpec((rank, rank), lambda i: (0, 0)),
        out_shape=jax.ShapeDtypeStruct((rank, rank), f32),
        cost_estimate=pl.CostEstimate(flops=40_000_000, bytes_accessed=131072, transcendentals=0),
    )(both)


def split(value):
    high = lax.reduce_precision(value, 8, 7)
    return high.astype(bf16), (value - high).astype(bf16)


def term_kernel(*refs):
    lefts, slices, inners, (out_ref, high_ref, low_ref, power_ref) = refs[:4], refs[4:8], refs[8:12], refs[12:]
    rows, rank = lefts[0].shape

    @pl.when(pl.program_id(0) == 0)
    def _():
        upd = [
            jnp.dot(s[...], m[:rank, :], preferred_element_type=f32)
            + jnp.dot(s[...], m[rank:, :], preferred_element_type=f32)
            for s, m in zip(slices, inners)
        ]
        top = [jnp.max(jnp.abs(u), axis=(0, 1), keepdims=True) for u in upd]
        top = jnp.maximum(jnp.maximum(top[0], top[1]), jnp.maximum(top[2], top[3]))
        power = jnp.floor(jnp.log(512.0 / jnp.maximum(top, 1e-30)) * 1.4426950408889634)
        power_ref[...] = jnp.broadcast_to(power, power_ref.shape)
        scale = jnp.exp(power * 0.6931471805599453)
        for d, u in enumerate(upd):
            value = u * scale
            high = value.astype(bf16)
            high_ref[:, d * rank:(d + 1) * rank] = high
            low_ref[:, d * rank:(d + 1) * rank] = (value - high.astype(f32)).astype(bf16)

    result = jnp.zeros((rows, high_ref.shape[0]), f32)
    for d, left in enumerate(lefts):
        for part_ref in (high_ref, low_ref):
            result += lax.dot_general(
                left[...], part_ref[:, d * rank:(d + 1) * rank], (((1,), (1,)), ((), ())), preferred_element_type=f32
            )
    out_ref[0, :rows, :] = result
    out_ref[0, rows:, :] = jnp.broadcast_to(power_ref[:1, :1], (NOTE, result.shape[1]))


def terms(lefts, inners, slices):
    part, rank = slices[0].shape
    order = NX * part
    rows = order // NZ

    def last(array):
        place = array.shape[0] // (2 * rank) - 1
        return pl.BlockSpec((2 * rank, rank), lambda i: (place, 0))

    return pl.pallas_call(
        term_kernel,
        grid=(NZ,),
        in_specs=[pl.BlockSpec((rows, rank), lambda i: (i, 0))] * 4
        + [pl.BlockSpec((part, rank), lambda i: (0, 0))] * 4
        + [last(m) for m in inners],
        out_specs=pl.BlockSpec((1, rows + NOTE, part), lambda i: (i, 0, 0)),
        out_shape=jax.ShapeDtypeStruct((NZ, rows + NOTE, part), f32),
        scratch_shapes=[
            pltpu.VMEM((part, NX * rank), bf16),
            pltpu.VMEM((part, NX * rank), bf16),
            pltpu.VMEM((8, 128), f32),
        ],
        cost_estimate=pl.CostEstimate(flops=2 * 2 * order * part * NX * rank, bytes_accessed=8 << 20, transcendentals=0),
        compiler_params=pltpu.CompilerParams(vmem_limit_bytes=24 << 20),
    )(*lefts, *slices, *inners)


def update_block(left, right, closing_left, closing_right, at_first, x, meanwhile):
    order, rank = left.shape
    part, rows = order // NX, order // NZ
    both = ("row", "col")
    next_right = lax.ppermute(jnp.where(at_first, closing_right, right), both, across(-1, 0))
    far = lax.ppermute(left, "col", along_x(2))
    given = jnp.where(at_first, closing_left, left)
    slices = [lax.dynamic_slice_in_dim(given, (x + d) % NX * part, part, 0) for d in range(NX)]
    slices = [lax.ppermute(slices[d], both, across(-1, d)) for d in range(NX)]
    inner = lax.dot_general(next_right, right, (((0,), (0,)), ((), ())), preferred_element_type=f32)
    inner = jnp.concatenate(split(inner), 0)
    packed = jnp.concatenate([left, inner], 0)
    packed, inner, far, *slices = lax.optimization_barrier((packed, inner, far, *slices))
    one, three = [lax.ppermute(packed, "col", along_x(d)) for d in (1, 3)]
    two = lax.ppermute(inner, "col", along_x(2))
    sent = terms((packed, one, far, three), (packed, one, two, three), slices).astype(f16)
    got = lax.all_to_all(sent, "col", 0, 0, axis_index_groups=Z_GROUPS, tiled=True)
    got, other = lax.optimization_barrier((got, meanwhile(sent)))
    got = got.astype(f32)
    return jnp.sum(got[:, :rows] * jnp.exp2(-got[:, rows:rows + 1, :1]), 0), other


def with_mate(half, even):
    other = lax.ppermute(half, "col", MATE)
    return jnp.concatenate([jnp.where(even, half, other), jnp.where(even, other, half)], 0)


def recompress(block, start, even):
    rows = block.shape[0]
    basis = start.astype(f32)
    factor = None
    for turn in range(SUB):
        image = lax.dot_general(block, basis, (((0,), (0,)), ((), ())), precision=HI)
        upper, lower = image[:rows], image[rows:]
        half = jnp.where(even, upper, lower) + lax.ppermute(jnp.where(even, lower, upper), "col", MATE)
        if factor is not None:
            half, factor = lax.optimization_barrier((half, factor))
        image = with_mate(total(half, along_z), even)
        if factor is not None:
            image = lax.dot_general(image, factor, (((1,), (1,)), ((), ())), precision=HI)
        gram = lax.dot_general(image, image, (((0,), (0,)), ((), ())), precision=HI)
        back = jnp.dot(block, image, precision=HI)
        both = total(jnp.concatenate([back, gram], 0), along_x)
        basis, both = lax.optimization_barrier((both[:rows], both))
        factor = inverse_factor(both, start.shape[1])
    dims = (((1,), (1,)), ((), ()))
    ortho = lax.dot_general(image, factor, dims, precision=HI)
    return ortho, lax.dot_general(with_mate(basis, even), factor, dims, precision=HI)


def local(
    left_factors,
    right_factors,
    closing_left,
    closing_right,
    panel_left,
    panel_right,
    diag_inverse,
    fronts,
):
    order, rank = panel_left.shape
    width = fronts.shape[1]
    col = lax.axis_index("col")
    x, z = col // NZ, col % NZ
    at_first = lax.axis_index("row") == 0
    rows = order // NZ
    even = z % 2 == 0

    def fixed_products(after):
        inverse, panel, _ = lax.optimization_barrier((diag_inverse, panel_left, after))
        right = jnp.concatenate([fronts, panel_right, from_behind(panel, "row", 1)], 1)
        return jnp.dot(inverse, right, preferred_element_type=f32)

    block, fixed = update_block(
        left_factors, right_factors, closing_left, closing_right, at_first, x, fixed_products
    )
    ortho, basis = recompress(block, lax.dynamic_slice_in_dim(panel_right, z * rows, rows, 0), even)
    sent = (-ortho).astype(bf16)
    prev_ortho = in_order([lax.ppermute(sent, ("row", "col"), across(1, d)) for d in range(NX)], x)
    basis = basis.astype(bf16)
    full_basis = in_order([basis] + [lax.ppermute(basis, "col", along_z(d)) for d in (1, 2, 3)], z // 2)
    late = jnp.dot(diag_inverse, jnp.concatenate([full_basis, prev_ortho], 1), preferred_element_type=f32)
    direct = fixed[:, :width]
    weights = jnp.concatenate([fixed[:, width:width + rank], late[:, :rank]], 1)
    carried = jnp.concatenate([fixed[:, width + rank:], late[:, rank:]], 1)
    seen = lax.dot_general(
        weights, jnp.concatenate([direct, carried], 1), (((0,), (0,)), ((), ())), precision=HI
    )
    offset, link = seen[:, :width], -seen[:, width:]
    short = link.astype(bf16)
    near = [(from_behind(short, "row", d), from_behind(offset, "row", d)) for d in (1, 2)]
    held = near[0][1] + jnp.dot(near[0][0].astype(f32), near[1][1], precision=HI)
    chain = jnp.dot(near[0][0], near[1][0], preferred_element_type=f32)
    far = (from_behind(chain.astype(bf16), "row", 2), from_behind(held, "row", 2))
    held = held + jnp.dot(chain, far[1], precision=HI)
    chain = jnp.dot(chain, far[0].astype(f32), precision=HI)
    incoming = held + jnp.dot(chain, from_behind(held, "row", 4), precision=HI)
    result = direct - jnp.dot(carried, incoming, precision=HI)
    return (result, offset + jnp.dot(link, incoming, precision=HI))


def solution(mesh):
    return jax.shard_map(
        local,
        mesh=mesh,
        in_specs=(
            P("row", "col"),
            P("row", "col"),
            P(None, "col"),
            P(None, "col"),
            P("row", None),
            P("row", None),
            P("row", None),
            P("row", "col"),
        ),
        out_specs=(P("row", "col"), P("row", "col")),
        check_vma=False,
    )
```

profile of v0, /device:TPU:16, one launch (start us, length us, event | category | flops | bytes accessed | tf_op | source)
XLA Modules:
  0.0 318.1 jit_solution(16807509899388450220)
XLA Ops:
  1.9 3.1 collective-permute-start.1
  9.1 1.6 collective-permute-start.2
  11.2 9.2 %collective-permute-done.5.refs_7_ = bf16[512,128]{1,0:T(8,128)(2,1)S(1)} collective-permute-done((bf16[512,128]{1,0:T(8,128)(2,1)S(1)}, bf16[512,128]{1,0:T(8,128)(2,1)S(1)}, u32[]{:S(2)}, u32[]{:S(2)}) %collective-permute-start.5) | collective-permute-done | bytes 131104 | tf_op jit(solution)/shard_map/ppermute | solution.py:165
  20.4 3.1 collective-permute-done.3.refs_5_
  23.5 2.4 collective-permute-start.7
  26.0 2.6 collective-permute-start.8
  28.6 15.0 %collective-permute-done.8.refs_10_ = bf16[256,128]{1,0:T(8,128)(2,1)S(1)} collective-permute-done((bf16[256,128]{1,0:T(8,128)(2,1)S(1)}, bf16[256,128]{1,0:T(8,128)(2,1)S(1)}, u32[]{:S(2)}, u32[]{:S(2)}) %collective-permute-start.8) | collective-permute-done | bytes 65568 | tf_op jit(solution)/shard_map/ppermute | solution.py:171
  44.5 6.6 %shard_map.95 = f32[8,272,512]{2,1,0:T(8,128)S(1)} custom-call(bf16[2304,128]{1,0:T(8,128)(2,1)S(1)} %pad_maximum_fusion.refs_0_.refs_8_, bf16[2304,128]{1,0:T(8,128)(2,1)S(1)} %collective-permute-done.6.refs_1_.refs_9_, bf16[2048,128]{1,0:T(8,128)(2,1)S(1)} %collective-permute-done.1.refs_2_, bf16[2304,128]{1,0:T(8,128)(2,1)S(1)} %collective-permute-done.7.refs_3_.refs_11_, ...), custom_call_target="tpu_custom_call" | custom-call | flops 2147483648 | bytes 8388608 | tf_op jit(solution)/shard_map/pallas_call | solution.py:139
  51.2 1.9 convert_element_type.29
  53.1 8.6 %all-to-all-start = ((f16[8,272,512]{2,1,0:T(8,128)(2,1)}), f16[8,272,512]{2,1,0:T(8,128)(2,1)S(1)}, u32[]{:S(2)}, u32[]{:S(2)}) async-start(f16[8,272,512]{2,1,0:T(8,128)(2,1)} %convert_element_type.29), calls=%async_computation | async-start | bytes 4456448 | tf_op jit(solution)/shard_map/all_to_all | solution.py:173
  61.7 2.1 collective-permute-start.9
  63.9 8.5 %collective-permute-done.9 = bf16[2048,128]{1,0:T(8,128)(2,1)} collective-permute-done((bf16[2048,128]{1,0:T(8,128)(2,1)S(1)}, bf16[2048,128]{1,0:T(8,128)(2,1)}, u32[]{:S(2)}, u32[]{:S(2)}) %collective-permute-start.9) | collective-permute-done | bytes 524320 | tf_op jit(solution)/shard_map/ppermute | solution.py:39
  72.3 9.7 %fusion.13 = f32[2048,384]{1,0:T(8,128)} fusion(bf16[2048,2048]{1,0:T(8,128)(2,1)} %param.14, bf16[2048,128]{1,0:T(8,128)(2,1)} %collective-permute-done.9, bf16[2048,128]{1,0:T(8,128)(2,1)S(1)} %copy-done.6, bf16[2048,128]{1,0:T(8,128)(2,1)} %param.15), kind=kOutput, calls=%fused_computation.16 | convolution fusion | flops 3225944064 | bytes 13107200 | tf_op jit(solution)/shard_map/dot_general | solution.py:228
  82.1 33.7 %all-to-all-done = f16[8,272,512]{2,1,0:T(8,128)(2,1)S(1)} async-done(((f16[8,272,512]{2,1,0:T(8,128)(2,1)}), f16[8,272,512]{2,1,0:T(8,128)(2,1)S(1)}, u32[]{:S(2)}, u32[]{:S(2)}) %all-to-all-start) | async-done | bytes 2228256 | tf_op jit(solution)/shard_map/all_to_all | solution.py:173
  118.4 4.4 %collective-permute-done.10 = f32[256,128]{1,0:T(8,128)S(1)} collective-permute-done((f32[256,128]{1,0:T(8,128)S(1)}, f32[256,128]{1,0:T(8,128)S(1)}, u32[]{:S(2)}, u32[]{:S(2)}) %collective-permute-start.10) | collective-permute-done | bytes 131104 | tf_op jit(solution)/shard_map/ppermute | solution.py:191
  123.8 2.1 collective-permute-start.12
  127.1 5.7 %collective-permute-done.13 = f32[256,128]{1,0:T(8,128)S(1)} collective-permute-done((f32[256,128]{1,0:T(8,128)S(1)}, f32[256,128]{1,0:T(8,128)S(1)}, u32[]{:S(2)}, u32[]{:S(2)}) %collective-permute-start.13) | collective-permute-done | bytes 131104 | tf_op jit(solution)/shard_map/ppermute | solution.py:43
  132.8 2.5 collective-permute-done.12
  135.3 4.2 %collective-permute-start.14 = (f32[256,128]{1,0:T(8,128)S(1)}, f32[256,128]{1,0:T(8,128)S(1)}, u32[]{:S(2)}, u32[]{:S(2)}) collective-permute-start(f32[256,128]{1,0:T(8,128)S(1)} %add_add_fusion.5), channel_id=1, source_target_pairs={{0,1},{1,0},{2,3},{3,2},{4,5},{5,4},{6,7},{7,6},{8,9},{9,8},{10,11... | collective-permute-start | bytes 393224 | tf_op jit(solution)/shard_map/ppermute | solution.py:180
  139.5 2.9 collective-permute-done.14
  143.8 3.2 %collective-permute-start.17 = (f32[384,128]{1,0:T(8,128)S(1)}, f32[384,128]{1,0:T(8,128)S(1)}, u32[]{:S(2)}, u32[]{:S(2)}) collective-permute-start(f32[384,128]{1,0:T(8,128)S(1)} %pad_maximum_fusion.4), channel_id=1, source_target_pairs={{0,24},{1,25},{2,26},{3,27},{4,28},{5,29},{6,30},{7,31},{8,0},{9,1... | collective-permute-start | bytes 589832 | tf_op jit(solution)/shard_map/ppermute | solution.py:43
  147.2 4.3 %collective-permute-done.16 = f32[384,128]{1,0:T(8,128)S(1)} collective-permute-done((f32[384,128]{1,0:T(8,128)S(1)}, f32[384,128]{1,0:T(8,128)S(1)}, u32[]{:S(2)}, u32[]{:S(2)}) %collective-permute-start.16) | collective-permute-done | bytes 196640 | tf_op jit(solution)/shard_map/ppermute | solution.py:43
  152.3 2.1 collective-permute-done.15
  155.5 2.1 collective-permute-start.18
  157.6 5.0 %shard_map.96 = f32[128,128]{1,0:T(8,128)} custom-call(f32[384,128]{1,0:T(8,128)} %copy-done.3), custom_call_target="tpu_custom_call" | custom-call | flops 40000000 | bytes 131072 | tf_op jit(solution)/shard_map/pallas_call | solution.py:83
  162.6 2.1 collective-permute-start.21
  165.6 2.6 collective-permute-start.19
  168.2 4.3 %collective-permute-done.21 = f32[256,128]{1,0:T(8,128)S(1)} collective-permute-done((f32[256,128]{1,0:T(8,128)S(1)}, f32[256,128]{1,0:T(8,128)S(1)}, u32[]{:S(2)}, u32[]{:S(2)}) %collective-permute-start.21) | collective-permute-done | bytes 131104 | tf_op jit(solution)/shard_map/ppermute | solution.py:43
  172.5 1.6 collective-permute-done.20
  174.1 4.6 %collective-permute-done.19 = f32[256,128]{1,0:T(8,128)S(1)} collective-permute-done((f32[256,128]{1,0:T(8,128)S(1)}, f32[256,128]{1,0:T(8,128)S(1)}, u32[]{:S(2)}, u32[]{:S(2)}) %collective-permute-start.19) | collective-permute-done | bytes 131104 | tf_op jit(solution)/shard_map/ppermute | solution.py:43
  178.9 5.0 %collective-permute-done.22 = f32[256,128]{1,0:T(8,128)S(1)} collective-permute-done((f32[256,128]{1,0:T(8,128)S(1)}, f32[256,128]{1,0:T(8,128)S(1)}, u32[]{:S(2)}, u32[]{:S(2)}) %collective-permute-start.22) | collective-permute-done | bytes 131104 | tf_op jit(solution)/shard_map/ppermute | solution.py:180
  186.4 3.2 %collective-permute-start.25 = (f32[384,128]{1,0:T(8,128)S(1)}, f32[384,128]{1,0:T(8,128)S(1)}, u32[]{:S(2)}, u32[]{:S(2)}) collective-permute-start(f32[384,128]{1,0:T(8,128)S(1)} %pad_maximum_fusion.5), channel_id=1, source_target_pairs={{0,24},{1,25},{2,26},{3,27},{4,28},{5,29},{6,30},{7,31},{8,0},{9,1... | collective-permute-start | bytes 589832 | tf_op jit(solution)/shard_map/ppermute | solution.py:43
  189.6 3.6 %collective-permute-done.24 = f32[384,128]{1,0:T(8,128)S(1)} collective-permute-done((f32[384,128]{1,0:T(8,128)S(1)}, f32[384,128]{1,0:T(8,128)S(1)}, u32[]{:S(2)}, u32[]{:S(2)}) %collective-permute-start.24) | collective-permute-done | bytes 196640 | tf_op jit(solution)/shard_map/ppermute | solution.py:43
  193.2 1.7 collective-permute-done.25
  194.9 1.9 collective-permute-done.23
  198.4 5.0 %shard_map.97 = f32[128,128]{1,0:T(8,128)} custom-call(f32[384,128]{1,0:T(8,128)} %copy-done.4), custom_call_target="tpu_custom_call" | custom-call | flops 40000000 | bytes 131072 | tf_op jit(solution)/shard_map/pallas_call | solution.py:83
  207.5 3.4 %collective-permute-start.27 = (f32[256,128]{1,0:T(8,128)S(1)}, f32[256,128]{1,0:T(8,128)S(1)}, u32[]{:S(2)}, u32[]{:S(2)}) collective-permute-start(f32[256,128]{1,0:T(8,128)S(1)} %select_add_fusion), channel_id=1, source_target_pairs={{0,4},{1,5},{2,6},{3,7},{4,0},{5,1},{6,2},{7,3},{8,12},{9,13},{10,... | collective-permute-start | bytes 393224 | tf_op jit(solution)/shard_map/ppermute | solution.py:43
  210.9 2.6 collective-permute-done.29
  214.4 4.2 %collective-permute-done.27 = f32[256,128]{1,0:T(8,128)S(1)} collective-permute-done((f32[256,128]{1,0:T(8,128)S(1)}, f32[256,128]{1,0:T(8,128)S(1)}, u32[]{:S(2)}, u32[]{:S(2)}) %collective-permute-start.27) | collective-permute-done | bytes 131104 | tf_op jit(solution)/shard_map/ppermute | solution.py:43
  218.9 4.8 %collective-permute-done.30 = f32[256,128]{1,0:T(8,128)S(1)} collective-permute-done((f32[256,128]{1,0:T(8,128)S(1)}, f32[256,128]{1,0:T(8,128)S(1)}, u32[]{:S(2)}, u32[]{:S(2)}) %collective-permute-start.30) | collective-permute-done | bytes 131104 | tf_op jit(solution)/shard_map/ppermute | solution.py:180
  226.3 3.2 %collective-permute-start.33 = (f32[384,128]{1,0:T(8,128)S(1)}, f32[384,128]{1,0:T(8,128)S(1)}, u32[]{:S(2)}, u32[]{:S(2)}) collective-permute-start(f32[384,128]{1,0:T(8,128)S(1)} %pad_maximum_fusion.6), channel_id=1, source_target_pairs={{0,24},{1,25},{2,26},{3,27},{4,28},{5,29},{6,30},{7,31},{8,0},{9,1... | collective-permute-start | bytes 589832 | tf_op jit(solution)/shard_map/ppermute | solution.py:43
  230.5 2.6 collective-permute-done.32
  233.1 1.7 collective-permute-done.33
  234.8 2.0 collective-permute-done.31
  237.5 5.0 %shard_map.98 = f32[128,128]{1,0:T(8,128)} custom-call(f32[384,128]{1,0:T(8,128)} %copy-done.5), custom_call_target="tpu_custom_call" | custom-call | flops 40000000 | bytes 131072 | tf_op jit(solution)/shard_map/pallas_call | solution.py:83
  243.9 1.9 collective-permute-start.41
  245.8 1.9 collective-permute-start.40
  247.8 3.7 %collective-permute-start.39 = (bf16[512,128]{1,0:T(8,128)(2,1)S(1)}, bf16[512,128]{1,0:T(8,128)(2,1)S(1)}, u32[]{:S(2)}, u32[]{:S(2)}) collective-permute-start(bf16[512,128]{1,0:T(8,128)(2,1)S(1)} %fusion.19), channel_id=1, source_target_pairs={{0,48},{1,49},{2,50},{3,51},{4,52},{5,53},{6,54},{7,55},{8,56},{9,... | collective-permute-start | bytes 393224 | tf_op jit(solution)/shard_map/ppermute | solution.py:235
  251.5 2.0 collective-permute-start.38
  254.8 3.5 %collective-permute-start.37 = (bf16[512,128]{1,0:T(8,128)(2,1)S(1)}, bf16[512,128]{1,0:T(8,128)(2,1)S(1)}, u32[]{:S(2)}, u32[]{:S(2)}) collective-permute-start(bf16[512,128]{1,0:T(8,128)(2,1)S(1)} %convolution_convert_fusion), channel_id=1, source_target_pairs={{0,2},{1,3},{2,4},{3,5},{4,6},{5,7},{6,0},{7,1},{8,10},{9,11},{10,... | collective-permute-start | bytes 393224 | tf_op jit(solution)/shard_map/ppermute | solution.py:237
  259.5 4.8 %collective-permute-start.36 = (bf16[512,128]{1,0:T(8,128)(2,1)S(1)}, bf16[512,128]{1,0:T(8,128)(2,1)S(1)}, u32[]{:S(2)}, u32[]{:S(2)}) collective-permute-start(bf16[512,128]{1,0:T(8,128)(2,1)S(1)} %convolution_convert_fusion), channel_id=1, source_target_pairs={{0,4},{1,5},{2,6},{3,7},{4,0},{5,1},{6,2},{7,3},{8,12},{9,13},{10,... | collective-permute-start | bytes 393224 | tf_op jit(solution)/shard_map/ppermute | solution.py:237
  264.4 2.1 collective-permute-start.35
  266.7 9.3 %collective-permute-done.35 = bf16[512,128]{1,0:T(8,128)(2,1)S(1)} collective-permute-done((bf16[512,128]{1,0:T(8,128)(2,1)S(1)}, bf16[512,128]{1,0:T(8,128)(2,1)S(1)}, u32[]{:S(2)}, u32[]{:S(2)}) %collective-permute-start.35) | collective-permute-done | bytes 131104 | tf_op jit(solution)/shard_map/ppermute | solution.py:237
  276.3 6.0 %convolution_bitcast_fusion = f32[2048,256]{1,0:T(8,128)S(1)} fusion(bf16[2048,2048]{1,0:T(8,128)(2,1)} %param.14, bf16[2048,128]{1,0:T(8,128)(2,1)S(1)} %constant_dynamic-slice_fusion, bf16[2048,128]{1,0:T(8,128)(2,1)S(1)} %constant_dynamic-slice_fusion.1), kind=kOutput, calls=%fused_computation.8 | convolution fusion | flops 2149580800 | bytes 11534336 | tf_op jit(solution)/shard_map/dot_general | solution.py:238
  282.7 3.7 %fusion.1 = f32[256,384]{1,0:T(8,128)S(1)} fusion(f32[2048,128]{1,0:T(8,128)S(1)} %get-tuple-element.65, f32[2048,128]{1,0:T(8,128)S(1)} %get-tuple-element.45, f32[2048,128]{1,0:T(8,128)S(1)} %get-tuple-element.46, f32[2048,128]{1,0:T(8,128)S(1)} %get-tuple-element.66, f32[2048,128]{1,0:T(8,128)S(1)} %get-tuple-element.44), kind=kOutput, calls=%fused_computation.2 | convolution fusion | flops 2418016256 | bytes 5636096 | tf_op jit(solution)/shard_map/dot_general | solution.py:242
  286.4 1.9 collective-permute-start.44
  288.3 1.9 collective-permute-start.42
  290.3 1.9 collective-permute-start.43
  292.2 1.9 collective-permute-start.45
  297.8 1.9 collective-permute-start.46
  300.8 1.9 collective-permute-start.47
  302.8 2.1 collective-permute-done.46
  308.0 5.6 %collective-permute-done.48 = f32[256,128]{1,0:T(8,128)S(1)} collective-permute-done((f32[256,128]{1,0:T(8,128)S(1)}, f32[256,128]{1,0:T(8,128)S(1)}, u32[]{:S(2)}, u32[]{:S(2)}) %collective-permute-start.48) | collective-permute-done | bytes 131104 | tf_op jit(solution)/shard_map/ppermute | solution.py:39
  314.0 2.8 convolution_subtract_fusion
  (130 shorter events, 43.4 us)
Async XLA Ops:
  0.6 10.1 %copy-start.1 = (bf16[2048,128]{1,0:T(8,128)(2,1)S(1)}, bf16[2048,128]{1,0:T(8,128)(2,1)}, u32[]{:S(2)}) copy-start(bf16[2048,128]{1,0:T(8,128)(2,1)} %param.9) | copy-start | bytes 1572868
  0.6 10.5 %copy-start.2 = (bf16[2048,128]{1,0:T(8,128)(2,1)S(1)}, bf16[2048,128]{1,0:T(8,128)(2,1)}, u32[]{:S(2)}) copy-start(bf16[2048,128]{1,0:T(8,128)(2,1)} %param.8) | copy-start | bytes 1572868
  1.9 7.3 %collective-permute-start = (bf16[2048,128]{1,0:T(8,128)(2,1)S(1)}, bf16[2048,128]{1,0:T(8,128)(2,1)S(1)}, u32[]{:S(2)}, u32[]{:S(2)}) collective-permute-start(bf16[2048,128]{1,0:T(8,128)(2,1)S(1)} %broadcast_select_fusion.1), channel_id=1, source_target_pairs={{0,224},{1,225},{2,226},{3,227},{4,228},{5,229},{6,230},{7,231},{8... | collective-permute-start | bytes 1572872 | tf_op jit(solution)/shard_map/ppermute | solution.py:161
  1.9 21.7 %collective-permute-start.1 = (bf16[2048,128]{1,0:T(8,128)(2,1)}, bf16[2048,128]{1,0:T(8,128)(2,1)S(1)}, u32[]{:S(2)}, u32[]{:S(2)}) collective-permute-start(bf16[2048,128]{1,0:T(8,128)(2,1)} %param.8), channel_id=1, source_target_pairs={{0,16},{1,17},{2,18},{3,19},{4,20},{5,21},{6,22},{7,23},{8,24},{9,... | collective-permute-start | bytes 1572872 | tf_op jit(solution)/shard_map/ppermute | solution.py:162
  6.2 14.2 %collective-permute-start.5 = (bf16[512,128]{1,0:T(8,128)(2,1)S(1)}, bf16[512,128]{1,0:T(8,128)(2,1)S(1)}, u32[]{:S(2)}, u32[]{:S(2)}) collective-permute-start(bf16[512,128]{1,0:T(8,128)(2,1)S(1)} %get-tuple-element.49), channel_id=1, source_target_pairs={{0,248},{1,249},{2,250},{3,251},{4,252},{5,253},{6,254},{7,255},{8... | collective-permute-start | bytes 393224 | tf_op jit(solution)/shard_map/ppermute | solution.py:165
  7.0 13.4 %collective-permute-start.4 = (bf16[512,128]{1,0:T(8,128)(2,1)S(1)}, bf16[512,128]{1,0:T(8,128)(2,1)S(1)}, u32[]{:S(2)}, u32[]{:S(2)}) collective-permute-start(bf16[512,128]{1,0:T(8,128)(2,1)S(1)} %get-tuple-element.50), channel_id=1, source_target_pairs={{0,240},{1,241},{2,242},{3,243},{4,244},{5,245},{6,246},{7,247},{8... | collective-permute-start | bytes 393224 | tf_op jit(solution)/shard_map/ppermute | solution.py:165
  8.5 15.0 %collective-permute-start.3 = (bf16[512,128]{1,0:T(8,128)(2,1)S(1)}, bf16[512,128]{1,0:T(8,128)(2,1)S(1)}, u32[]{:S(2)}, u32[]{:S(2)}) collective-permute-start(bf16[512,128]{1,0:T(8,128)(2,1)S(1)} %get-tuple-element.51), channel_id=1, source_target_pairs={{0,232},{1,233},{2,234},{3,235},{4,236},{5,237},{6,238},{7,239},{8... | collective-permute-start | bytes 393224 | tf_op jit(solution)/shard_map/ppermute | solution.py:165
  9.1 14.4 %collective-permute-start.2 = (bf16[512,128]{1,0:T(8,128)(2,1)S(1)}, bf16[512,128]{1,0:T(8,128)(2,1)S(1)}, u32[]{:S(2)}, u32[]{:S(2)}) collective-permute-start(bf16[512,128]{1,0:T(8,128)(2,1)S(1)} %get-tuple-element.52), channel_id=1, source_target_pairs={{0,224},{1,225},{2,226},{3,227},{4,228},{5,229},{6,230},{7,231},{8... | collective-permute-start | bytes 393224 | tf_op jit(solution)/shard_map/ppermute | solution.py:165
  23.5 20.0 %collective-permute-start.7 = (bf16[2304,128]{1,0:T(8,128)(2,1)S(1)}, bf16[2304,128]{1,0:T(8,128)(2,1)S(1)}, u32[]{:S(2)}, u32[]{:S(2)}) collective-permute-start(bf16[2304,128]{1,0:T(8,128)(2,1)S(1)} %pad_maximum_fusion.refs_0_.refs_8_), channel_id=1, source_target_pairs={{0,24},{1,25},{2,26},{3,27},{4,28},{5,29},{6,30},{7,31},{8,0},{9,1... | collective-permute-start | bytes 1769480 | tf_op jit(solution)/shard_map/ppermute | solution.py:170
  26.0 18.6 %collective-permute-start.6 = (bf16[2304,128]{1,0:T(8,128)(2,1)S(1)}, bf16[2304,128]{1,0:T(8,128)(2,1)S(1)}, u32[]{:S(2)}, u32[]{:S(2)}) collective-permute-start(bf16[2304,128]{1,0:T(8,128)(2,1)S(1)} %pad_maximum_fusion.refs_0_.refs_8_), channel_id=1, source_target_pairs={{0,8},{1,9},{2,10},{3,11},{4,12},{5,13},{6,14},{7,15},{8,16},{9,17... | collective-permute-start | bytes 1769480 | tf_op jit(solution)/shard_map/ppermute | solution.py:170
  26.0 17.6 %collective-permute-start.8 = (bf16[256,128]{1,0:T(8,128)(2,1)S(1)}, bf16[256,128]{1,0:T(8,128)(2,1)S(1)}, u32[]{:S(2)}, u32[]{:S(2)}) collective-permute-start(bf16[256,128]{1,0:T(8,128)(2,1)S(1)} %pad_maximum_fusion.7), channel_id=1, source_target_pairs={{0,16},{1,17},{2,18},{3,19},{4,20},{5,21},{6,22},{7,23},{8,24},{9,... | collective-permute-start | bytes 196616 | tf_op jit(solution)/shard_map/ppermute | solution.py:171
  53.1 8.6 %copy-start.7 = (bf16[2048,128]{1,0:T(8,128)(2,1)S(1)}, bf16[2048,128]{1,0:T(8,128)(2,1)}, u32[]{:S(2)}) copy-start(bf16[2048,128]{1,0:T(8,128)(2,1)} %param.12) | copy-start | bytes 1572868
  53.1 19.2 %copy-start.6 = (bf16[2048,128]{1,0:T(8,128)(2,1)S(1)}, bf16[2048,128]{1,0:T(8,128)(2,1)}, u32[]{:S(2)}) copy-start(bf16[2048,128]{1,0:T(8,128)(2,1)} %param.13) | copy-start | bytes 1572868
  53.1 62.6 %all-to-all-start = ((f16[8,272,512]{2,1,0:T(8,128)(2,1)}), f16[8,272,512]{2,1,0:T(8,128)(2,1)S(1)}, u32[]{:S(2)}, u32[]{:S(2)}) async-start(f16[8,272,512]{2,1,0:T(8,128)(2,1)} %convert_element_type.29), calls=%async_computation | async-start | bytes 4456448 | tf_op jit(solution)/shard_map/all_to_all | solution.py:173
  61.7 10.6 %collective-permute-start.9 = (bf16[2048,128]{1,0:T(8,128)(2,1)S(1)}, bf16[2048,128]{1,0:T(8,128)(2,1)}, u32[]{:S(2)}, u32[]{:S(2)}) collective-permute-start(bf16[2048,128]{1,0:T(8,128)(2,1)S(1)} %copy-done.7), channel_id=1, source_target_pairs={{0,32},{32,64},{64,96},{96,128},{128,160},{160,192},{192,224},{1,3... | collective-permute-start | bytes 1572872 | tf_op jit(solution)/shard_map/ppermute | solution.py:39
  117.8 5.1 %collective-permute-start.10 = (f32[256,128]{1,0:T(8,128)S(1)}, f32[256,128]{1,0:T(8,128)S(1)}, u32[]{:S(2)}, u32[]{:S(2)}) collective-permute-start(f32[256,128]{1,0:T(8,128)S(1)} %slice_select_fusion.2), channel_id=1, source_target_pairs={{0,1},{1,0},{2,3},{3,2},{4,5},{5,4},{6,7},{7,6},{8,9},{9,8},{10,11... | collective-permute-start | bytes 393224 | tf_op jit(solution)/shard_map/ppermute | solution.py:191
  122.9 9.9 %collective-permute-start.13 = (f32[256,128]{1,0:T(8,128)S(1)}, f32[256,128]{1,0:T(8,128)S(1)}, u32[]{:S(2)}, u32[]{:S(2)}) collective-permute-start(f32[256,128]{1,0:T(8,128)S(1)} %select_add_fusion.2), channel_id=1, source_target_pairs={{0,6},{1,7},{2,0},{3,1},{4,2},{5,3},{6,4},{7,5},{8,14},{9,15},{10,... | collective-permute-start | bytes 393224 | tf_op jit(solution)/shard_map/ppermute | solution.py:43
  123.8 11.5 %collective-permute-start.12 = (f32[256,128]{1,0:T(8,128)S(1)}, f32[256,128]{1,0:T(8,128)S(1)}, u32[]{:S(2)}, u32[]{:S(2)}) collective-permute-start(f32[256,128]{1,0:T(8,128)S(1)} %select_add_fusion.2), channel_id=1, source_target_pairs={{0,2},{1,3},{2,4},{3,5},{4,6},{5,7},{6,0},{7,1},{8,10},{9,11},{10,... | collective-permute-start | bytes 393224 | tf_op jit(solution)/shard_map/ppermute | solution.py:43
  125.9 9.4 %collective-permute-start.11 = (f32[256,128]{1,0:T(8,128)S(1)}, f32[256,128]{1,0:T(8,128)S(1)}, u32[]{:S(2)}, u32[]{:S(2)}) collective-permute-start(f32[256,128]{1,0:T(8,128)S(1)} %select_add_fusion.2), channel_id=1, source_target_pairs={{0,4},{1,5},{2,6},{3,7},{4,0},{5,1},{6,2},{7,3},{8,12},{9,13},{10,... | collective-permute-start | bytes 393224 | tf_op jit(solution)/shard_map/ppermute | solution.py:43
  135.3 7.1 %collective-permute-start.14 = (f32[256,128]{1,0:T(8,128)S(1)}, f32[256,128]{1,0:T(8,128)S(1)}, u32[]{:S(2)}, u32[]{:S(2)}) collective-permute-start(f32[256,128]{1,0:T(8,128)S(1)} %add_add_fusion.5), channel_id=1, source_target_pairs={{0,1},{1,0},{2,3},{3,2},{4,5},{5,4},{6,7},{7,6},{8,9},{9,8},{10,11... | collective-permute-start | bytes 393224 | tf_op jit(solution)/shard_map/ppermute | solution.py:180
  143.7 7.9 %collective-permute-start.16 = (f32[384,128]{1,0:T(8,128)S(1)}, f32[384,128]{1,0:T(8,128)S(1)}, u32[]{:S(2)}, u32[]{:S(2)}) collective-permute-start(f32[384,128]{1,0:T(8,128)S(1)} %pad_maximum_fusion.4), channel_id=1, source_target_pairs={{0,8},{1,9},{2,10},{3,11},{4,12},{5,13},{6,14},{7,15},{8,16},{9,17... | collective-permute-start | bytes 589832 | tf_op jit(solution)/shard_map/ppermute | solution.py:43
  143.8 8.5 %collective-permute-start.17 = (f32[384,128]{1,0:T(8,128)S(1)}, f32[384,128]{1,0:T(8,128)S(1)}, u32[]{:S(2)}, u32[]{:S(2)}) collective-permute-start(f32[384,128]{1,0:T(8,128)S(1)} %pad_maximum_fusion.4), channel_id=1, source_target_pairs={{0,24},{1,25},{2,26},{3,27},{4,28},{5,29},{6,30},{7,31},{8,0},{9,1... | collective-permute-start | bytes 589832 | tf_op jit(solution)/shard_map/ppermute | solution.py:43
  147.0 7.4 %collective-permute-start.15 = (f32[384,128]{1,0:T(8,128)S(1)}, f32[384,128]{1,0:T(8,128)S(1)}, u32[]{:S(2)}, u32[]{:S(2)}) collective-permute-start(f32[384,128]{1,0:T(8,128)S(1)} %pad_maximum_fusion.4), channel_id=1, source_target_pairs={{0,16},{1,17},{2,18},{3,19},{4,20},{5,21},{6,22},{7,23},{8,24},{9,... | collective-permute-start | bytes 589832 | tf_op jit(solution)/shard_map/ppermute | solution.py:43
  154.4 3.2 copy-start.3
  155.5 7.1 %collective-permute-start.18 = (f32[256,128]{1,0:T(8,128)S(1)}, f32[256,128]{1,0:T(8,128)S(1)}, u32[]{:S(2)}, u32[]{:S(2)}) collective-permute-start(f32[256,128]{1,0:T(8,128)S(1)} %slice_select_fusion.1), channel_id=1, source_target_pairs={{0,1},{1,0},{2,3},{3,2},{4,5},{5,4},{6,7},{7,6},{8,9},{9,8},{10,11... | collective-permute-start | bytes 393224 | tf_op jit(solution)/shard_map/ppermute | solution.py:191
  162.6 9.9 %collective-permute-start.21 = (f32[256,128]{1,0:T(8,128)S(1)}, f32[256,128]{1,0:T(8,128)S(1)}, u32[]{:S(2)}, u32[]{:S(2)}) collective-permute-start(f32[256,128]{1,0:T(8,128)S(1)} %select_add_fusion.1), channel_id=1, source_target_pairs={{0,6},{1,7},{2,0},{3,1},{4,2},{5,3},{6,4},{7,5},{8,14},{9,15},{10,... | collective-permute-start | bytes 393224 | tf_op jit(solution)/shard_map/ppermute | solution.py:43
  164.7 9.5 %collective-permute-start.20 = (f32[256,128]{1,0:T(8,128)S(1)}, f32[256,128]{1,0:T(8,128)S(1)}, u32[]{:S(2)}, u32[]{:S(2)}) collective-permute-start(f32[256,128]{1,0:T(8,128)S(1)} %select_add_fusion.1), channel_id=1, source_target_pairs={{0,2},{1,3},{2,4},{3,5},{4,6},{5,7},{6,0},{7,1},{8,10},{9,11},{10,... | collective-permute-start | bytes 393224 | tf_op jit(solution)/shard_map/ppermute | solution.py:43
  165.6 13.1 %collective-permute-start.19 = (f32[256,128]{1,0:T(8,128)S(1)}, f32[256,128]{1,0:T(8,128)S(1)}, u32[]{:S(2)}, u32[]{:S(2)}) collective-permute-start(f32[256,128]{1,0:T(8,128)S(1)} %select_add_fusion.1), channel_id=1, source_target_pairs={{0,4},{1,5},{2,6},{3,7},{4,0},{5,1},{6,2},{7,3},{8,12},{9,13},{10,... | collective-permute-start | bytes 393224 | tf_op jit(solution)/shard_map/ppermute | solution.py:43
  178.8 5.1 %collective-permute-start.22 = (f32[256,128]{1,0:T(8,128)S(1)}, f32[256,128]{1,0:T(8,128)S(1)}, u32[]{:S(2)}, u32[]{:S(2)}) collective-permute-start(f32[256,128]{1,0:T(8,128)S(1)} %add_add_fusion.4), channel_id=1, source_target_pairs={{0,1},{1,0},{2,3},{3,2},{4,5},{5,4},{6,7},{7,6},{8,9},{9,8},{10,11... | collective-permute-start | bytes 393224 | tf_op jit(solution)/shard_map/ppermute | solution.py:180
  186.3 7.0 %collective-permute-start.24 = (f32[384,128]{1,0:T(8,128)S(1)}, f32[384,128]{1,0:T(8,128)S(1)}, u32[]{:S(2)}, u32[]{:S(2)}) collective-permute-start(f32[384,128]{1,0:T(8,128)S(1)} %pad_maximum_fusion.5), channel_id=1, source_target_pairs={{0,8},{1,9},{2,10},{3,11},{4,12},{5,13},{6,14},{7,15},{8,16},{9,17... | collective-permute-start | bytes 589832 | tf_op jit(solution)/shard_map/ppermute | solution.py:43
  186.4 8.5 %collective-permute-start.25 = (f32[384,128]{1,0:T(8,128)S(1)}, f32[384,128]{1,0:T(8,128)S(1)}, u32[]{:S(2)}, u32[]{:S(2)}) collective-permute-start(f32[384,128]{1,0:T(8,128)S(1)} %pad_maximum_fusion.5), channel_id=1, source_target_pairs={{0,24},{1,25},{2,26},{3,27},{4,28},{5,29},{6,30},{7,31},{8,0},{9,1... | collective-permute-start | bytes 589832 | tf_op jit(solution)/shard_map/ppermute | solution.py:43
  189.6 7.2 %collective-permute-start.23 = (f32[384,128]{1,0:T(8,128)S(1)}, f32[384,128]{1,0:T(8,128)S(1)}, u32[]{:S(2)}, u32[]{:S(2)}) collective-permute-start(f32[384,128]{1,0:T(8,128)S(1)} %pad_maximum_fusion.5), channel_id=1, source_target_pairs={{0,16},{1,17},{2,18},{3,19},{4,20},{5,21},{6,22},{7,23},{8,24},{9,... | collective-permute-start | bytes 589832 | tf_op jit(solution)/shard_map/ppermute | solution.py:43
  196.8 1.6 copy-start.4
  197.9 6.6 %collective-permute-start.26 = (f32[256,128]{1,0:T(8,128)S(1)}, f32[256,128]{1,0:T(8,128)S(1)}, u32[]{:S(2)}, u32[]{:S(2)}) collective-permute-start(f32[256,128]{1,0:T(8,128)S(1)} %slice_select_fusion), channel_id=1, source_target_pairs={{0,1},{1,0},{2,3},{3,2},{4,5},{5,4},{6,7},{7,6},{8,9},{9,8},{10,11... | collective-permute-start | bytes 393224 | tf_op jit(solution)/shard_map/ppermute | solution.py:191
  204.5 9.0 %collective-permute-start.29 = (f32[256,128]{1,0:T(8,128)S(1)}, f32[256,128]{1,0:T(8,128)S(1)}, u32[]{:S(2)}, u32[]{:S(2)}) collective-permute-start(f32[256,128]{1,0:T(8,128)S(1)} %select_add_fusion), channel_id=1, source_target_pairs={{0,6},{1,7},{2,0},{3,1},{4,2},{5,3},{6,4},{7,5},{8,14},{9,15},{10,... | collective-permute-start | bytes 393224 | tf_op jit(solution)/shard_map/ppermute | solution.py:43
  206.0 8.4 %collective-permute-start.28 = (f32[256,128]{1,0:T(8,128)S(1)}, f32[256,128]{1,0:T(8,128)S(1)}, u32[]{:S(2)}, u32[]{:S(2)}) collective-permute-start(f32[256,128]{1,0:T(8,128)S(1)} %select_add_fusion), channel_id=1, source_target_pairs={{0,2},{1,3},{2,4},{3,5},{4,6},{5,7},{6,0},{7,1},{8,10},{9,11},{10,... | collective-permute-start | bytes 393224 | tf_op jit(solution)/shard_map/ppermute | solution.py:43
  207.5 11.1 %collective-permute-start.27 = (f32[256,128]{1,0:T(8,128)S(1)}, f32[256,128]{1,0:T(8,128)S(1)}, u32[]{:S(2)}, u32[]{:S(2)}) collective-permute-start(f32[256,128]{1,0:T(8,128)S(1)} %select_add_fusion), channel_id=1, source_target_pairs={{0,4},{1,5},{2,6},{3,7},{4,0},{5,1},{6,2},{7,3},{8,12},{9,13},{10,... | collective-permute-start | bytes 393224 | tf_op jit(solution)/shard_map/ppermute | solution.py:43
  218.7 5.1 %collective-permute-start.30 = (f32[256,128]{1,0:T(8,128)S(1)}, f32[256,128]{1,0:T(8,128)S(1)}, u32[]{:S(2)}, u32[]{:S(2)}) collective-permute-start(f32[256,128]{1,0:T(8,128)S(1)} %add_add_fusion.3), channel_id=1, source_target_pairs={{0,1},{1,0},{2,3},{3,2},{4,5},{5,4},{6,7},{7,6},{8,9},{9,8},{10,11... | collective-permute-start | bytes 393224 | tf_op jit(solution)/shard_map/ppermute | solution.py:180
  226.2 7.0 %collective-permute-start.32 = (f32[384,128]{1,0:T(8,128)S(1)}, f32[384,128]{1,0:T(8,128)S(1)}, u32[]{:S(2)}, u32[]{:S(2)}) collective-permute-start(f32[384,128]{1,0:T(8,128)S(1)} %pad_maximum_fusion.6), channel_id=1, source_target_pairs={{0,8},{1,9},{2,10},{3,11},{4,12},{5,13},{6,14},{7,15},{8,16},{9,17... | collective-permute-start | bytes 589832 | tf_op jit(solution)/shard_map/ppermute | solution.py:43
  226.3 8.5 %collective-permute-start.33 = (f32[384,128]{1,0:T(8,128)S(1)}, f32[384,128]{1,0:T(8,128)S(1)}, u32[]{:S(2)}, u32[]{:S(2)}) collective-permute-start(f32[384,128]{1,0:T(8,128)S(1)} %pad_maximum_fusion.6), channel_id=1, source_target_pairs={{0,24},{1,25},{2,26},{3,27},{4,28},{5,29},{6,30},{7,31},{8,0},{9,1... | collective-permute-start | bytes 589832 | tf_op jit(solution)/shard_map/ppermute | solution.py:43
  229.5 7.3 %collective-permute-start.31 = (f32[384,128]{1,0:T(8,128)S(1)}, f32[384,128]{1,0:T(8,128)S(1)}, u32[]{:S(2)}, u32[]{:S(2)}) collective-permute-start(f32[384,128]{1,0:T(8,128)S(1)} %pad_maximum_fusion.6), channel_id=1, source_target_pairs={{0,16},{1,17},{2,18},{3,19},{4,20},{5,21},{6,22},{7,23},{8,24},{9,... | collective-permute-start | bytes 589832 | tf_op jit(solution)/shard_map/ppermute | solution.py:43
  236.9 0.7 copy-start.5
  242.5 11.0 %collective-permute-start.34 = (f32[256,128]{1,0:T(8,128)S(1)}, f32[256,128]{1,0:T(8,128)S(1)}, u32[]{:S(2)}, u32[]{:S(2)}) collective-permute-start(f32[256,128]{1,0:T(8,128)S(1)} %slice.82), channel_id=1, source_target_pairs={{0,1},{1,0},{2,3},{3,2},{4,5},{5,4},{6,7},{7,6},{8,9},{9,8},{10,11... | collective-permute-start | bytes 393224 | tf_op jit(solution)/shard_map/ppermute | solution.py:180
  243.9 22.7 %collective-permute-start.41 = (bf16[512,128]{1,0:T(8,128)(2,1)S(1)}, bf16[512,128]{1,0:T(8,128)(2,1)S(1)}, u32[]{:S(2)}, u32[]{:S(2)}) collective-permute-start(bf16[512,128]{1,0:T(8,128)(2,1)S(1)} %fusion.19), channel_id=1, source_target_pairs={{0,32},{1,33},{2,34},{3,35},{4,36},{5,37},{6,38},{7,39},{8,40},{9,... | collective-permute-start | bytes 393224 | tf_op jit(solution)/shard_map/ppermute | solution.py:235
  245.8 20.7 %collective-permute-start.40 = (bf16[512,128]{1,0:T(8,128)(2,1)S(1)}, bf16[512,128]{1,0:T(8,128)(2,1)S(1)}, u32[]{:S(2)}, u32[]{:S(2)}) collective-permute-start(bf16[512,128]{1,0:T(8,128)(2,1)S(1)} %fusion.19), channel_id=1, source_target_pairs={{0,40},{1,41},{2,42},{3,43},{4,44},{5,45},{6,46},{7,47},{8,48},{9,... | collective-permute-start | bytes 393224 | tf_op jit(solution)/shard_map/ppermute | solution.py:235
  247.8 16.6 %collective-permute-start.39 = (bf16[512,128]{1,0:T(8,128)(2,1)S(1)}, bf16[512,128]{1,0:T(8,128)(2,1)S(1)}, u32[]{:S(2)}, u32[]{:S(2)}) collective-permute-start(bf16[512,128]{1,0:T(8,128)(2,1)S(1)} %fusion.19), channel_id=1, source_target_pairs={{0,48},{1,49},{2,50},{3,51},{4,52},{5,53},{6,54},{7,55},{8,56},{9,... | collective-permute-start | bytes 393224 | tf_op jit(solution)/shard_map/ppermute | solution.py:235
  251.5 8.0 %collective-permute-start.38 = (bf16[512,128]{1,0:T(8,128)(2,1)S(1)}, bf16[512,128]{1,0:T(8,128)(2,1)S(1)}, u32[]{:S(2)}, u32[]{:S(2)}) collective-permute-start(bf16[512,128]{1,0:T(8,128)(2,1)S(1)} %fusion.19), channel_id=1, source_target_pairs={{0,56},{1,57},{2,58},{3,59},{4,60},{5,61},{6,62},{7,63},{8,32},{9,... | collective-permute-start | bytes 393224 | tf_op jit(solution)/shard_map/ppermute | solution.py:235
  254.8 21.3 %collective-permute-start.37 = (bf16[512,128]{1,0:T(8,128)(2,1)S(1)}, bf16[512,128]{1,0:T(8,128)(2,1)S(1)}, u32[]{:S(2)}, u32[]{:S(2)}) collective-permute-start(bf16[512,128]{1,0:T(8,128)(2,1)S(1)} %convolution_convert_fusion), channel_id=1, source_target_pairs={{0,2},{1,3},{2,4},{3,5},{4,6},{5,7},{6,0},{7,1},{8,10},{9,11},{10,... | collective-permute-start | bytes 393224 | tf_op jit(solution)/shard_map/ppermute | solution.py:237
  259.5 16.5 %collective-permute-start.36 = (bf16[512,128]{1,0:T(8,128)(2,1)S(1)}, bf16[512,128]{1,0:T(8,128)(2,1)S(1)}, u32[]{:S(2)}, u32[]{:S(2)}) collective-permute-start(bf16[512,128]{1,0:T(8,128)(2,1)S(1)} %convolution_convert_fusion), channel_id=1, source_target_pairs={{0,4},{1,5},{2,6},{3,7},{4,0},{5,1},{6,2},{7,3},{8,12},{9,13},{10,... | collective-permute-start | bytes 393224 | tf_op jit(solution)/shard_map/ppermute | solution.py:237
  264.4 11.7 %collective-permute-start.35 = (bf16[512,128]{1,0:T(8,128)(2,1)S(1)}, bf16[512,128]{1,0:T(8,128)(2,1)S(1)}, u32[]{:S(2)}, u32[]{:S(2)}) collective-permute-start(bf16[512,128]{1,0:T(8,128)(2,1)S(1)} %convolution_convert_fusion), channel_id=1, source_target_pairs={{0,6},{1,7},{2,0},{3,1},{4,2},{5,3},{6,4},{7,5},{8,14},{9,15},{10,... | collective-permute-start | bytes 393224 | tf_op jit(solution)/shard_map/ppermute | solution.py:237
  276.3 6.0 %copy-start = (f32[2048,384]{1,0:T(8,128)S(1)}, f32[2048,384]{1,0:T(8,128)}, u32[]{:S(2)}) copy-start(f32[2048,384]{1,0:T(8,128)} %fusion.13) | copy-start | bytes 9437188
  286.4 9.1 %collective-permute-start.44 = (f32[256,128]{1,0:T(8,128)S(1)}, f32[256,128]{1,0:T(8,128)S(1)}, u32[]{:S(2)}, u32[]{:S(2)}) collective-permute-start(f32[256,128]{1,0:T(8,128)S(1)} %slice.85), channel_id=1, source_target_pairs={{0,64},{32,96},{64,128},{96,160},{128,192},{160,224},{1,65},{33,97... | collective-permute-start | bytes 393224 | tf_op jit(solution)/shard_map/ppermute | solution.py:39
  288.3 7.7 %collective-permute-start.42 = (f32[256,128]{1,0:T(8,128)S(1)}, f32[256,128]{1,0:T(8,128)S(1)}, u32[]{:S(2)}, u32[]{:S(2)}) collective-permute-start(f32[256,128]{1,0:T(8,128)S(1)} %slice.85), channel_id=1, source_target_pairs={{0,32},{32,64},{64,96},{96,128},{128,160},{160,192},{192,224},{1,3... | collective-permute-start | bytes 393224 | tf_op jit(solution)/shard_map/ppermute | solution.py:39
  290.3 7.2 %collective-permute-start.43 = (bf16[256,256]{1,0:T(8,128)(2,1)S(1)}, bf16[256,256]{1,0:T(8,128)(2,1)S(1)}, u32[]{:S(2)}, u32[]{:S(2)}) collective-permute-start(bf16[256,256]{1,0:T(8,128)(2,1)S(1)} %fusion.34), channel_id=1, source_target_pairs={{0,32},{32,64},{64,96},{96,128},{128,160},{160,192},{192,224},{1,3... | collective-permute-start | bytes 393224 | tf_op jit(solution)/shard_map/ppermute | solution.py:39
  292.2 8.4 %collective-permute-start.45 = (bf16[256,256]{1,0:T(8,128)(2,1)S(1)}, bf16[256,256]{1,0:T(8,128)(2,1)S(1)}, u32[]{:S(2)}, u32[]{:S(2)}) collective-permute-start(bf16[256,256]{1,0:T(8,128)(2,1)S(1)} %fusion.34), channel_id=1, source_target_pairs={{0,64},{32,96},{64,128},{96,160},{128,192},{160,224},{1,65},{33,97... | collective-permute-start | bytes 393224 | tf_op jit(solution)/shard_map/ppermute | solution.py:39
  297.8 7.1 %collective-permute-start.46 = (f32[256,128]{1,0:T(8,128)S(1)}, f32[256,128]{1,0:T(8,128)S(1)}, u32[]{:S(2)}, u32[]{:S(2)}) collective-permute-start(f32[256,128]{1,0:T(8,128)S(1)} %convolution_add_fusion.3), channel_id=1, source_target_pairs={{0,64},{32,96},{64,128},{96,160},{128,192},{160,224},{1,65},{33,97... | collective-permute-start | bytes 393224 | tf_op jit(solution)/shard_map/ppermute | solution.py:39
  300.8 6.9 %collective-permute-start.47 = (bf16[256,256]{1,0:T(8,128)(2,1)S(1)}, bf16[256,256]{1,0:T(8,128)(2,1)S(1)}, u32[]{:S(2)}, u32[]{:S(2)}) collective-permute-start(bf16[256,256]{1,0:T(8,128)(2,1)S(1)} %get-tuple-element.63), channel_id=1, source_target_pairs={{0,64},{32,96},{64,128},{96,160},{128,192},{160,224},{1,65},{33,97... | collective-permute-start | bytes 393224 | tf_op jit(solution)/shard_map/ppermute | solution.py:39
  305.2 8.4 %collective-permute-start.48 = (f32[256,128]{1,0:T(8,128)S(1)}, f32[256,128]{1,0:T(8,128)S(1)}, u32[]{:S(2)}, u32[]{:S(2)}) collective-permute-start(f32[256,128]{1,0:T(8,128)S(1)} %convolution_add_fusion.2), channel_id=1, source_target_pairs={{0,128},{32,160},{64,192},{96,224},{1,129},{33,161},{65,193},{97,2... | collective-permute-start | bytes 393224 | tf_op jit(solution)/shard_map/ppermute | solution.py:39
where the time goes:
time: 324 us; the launch traced here: 318 us
  waiting for transfers between devices  159 us (49%)
  starting transfers between devices  91.6 us (28%)
  matrix products  36.1 us (11%)
  Pallas kernels  21.7 us (7%)
  other arithmetic  6.12 us (2%)
    ppermute x18, waiting for transfers between devices, total(): got = [lax.ppermute(block, 'col', route(d)) for d in (2, 1, 3)]  47.1 us
    all_to_all x1, waiting for transfers between devices, update_block(): lax.all_to_all(sent, 'col', 0, 0, axis_index_groups=Z_GROUPS, tiled=True)  33.7 us
    ppermute x18, starting transfers between devices, total(): got = [lax.ppermute(block, 'col', route(d)) for d in (2, 1, 3)]  27.3 us
    ppermute x8, waiting for transfers between devices, from_behind(): return lax.ppermute(block, axis, route)  21.6 us
    pallas_call x3, Pallas kernels, inverse_factor(): pl.pallas_call(inverse_factor_kernel, grid=(1,), in_specs=[pl.BlockSpec((...  15 us
    ppermute x1, waiting for transfers between devices, update_block(): two = lax.ppermute(inner, 'col', along_x(2))  15 us
    ppermute x8, starting transfers between devices, from_behind(): return lax.ppermute(block, axis, route)  14.9 us
    ppermute x4, waiting for transfers between devices, with_mate(): other = lax.ppermute(half, 'col', MATE)  12.7 us
  transfers between devices with their start and end apart: 50, of which 37 were waited for; matrix products, arithmetic and copies ran while one was open for 5% of the time, Pallas kernels for 3%

commit v1 on v0

--- a/solution.py
+++ b/solution.py
@@ -243,11 +243,15 @@
         weights, jnp.concatenate([direct, carried], 1), (((0,), (0,)), ((), ())), precision=HI
     )
     offset, link = seen[:, :width], -seen[:, width:]
-    short = link.astype(bf16)
-    near = [(from_behind(short, "row", d), from_behind(offset, "row", d)) for d in (1, 2)]
-    held = near[0][1] + jnp.dot(near[0][0].astype(f32), near[1][1], precision=HI)
-    chain = jnp.dot(near[0][0], near[1][0], preferred_element_type=f32)
-    far = (from_behind(chain.astype(bf16), "row", 2), from_behind(held, "row", 2))
+    def maps(chain, held, distances):
+        packed = jnp.concatenate([chain.astype(bf16), *split(held)], 1)
+        got = [from_behind(packed, "row", d) for d in distances]
+        return [(g[:, :2 * rank], g[:, 2 * rank:-width].astype(f32) + g[:, -width:].astype(f32)) for g in got]
+
+    near, next_near = maps(link, offset, (1, 2))
+    held = near[1] + jnp.dot(near[0].astype(f32), next_near[1], precision=HI)
+    chain = jnp.dot(near[0], next_near[0], preferred_element_type=f32)
+    far, = maps(chain, held, (2,))
     held = held + jnp.dot(chain, far[1], precision=HI)
     chain = jnp.dot(chain, far[0].astype(f32), precision=HI)
     incoming = held + jnp.dot(chain, from_behind(held, "row", 4), precision=HI)

time: 324 us -> 336 us (1.037)
  waiting for transfers between devices: 159 us -> 169 us
  starting transfers between devices: 91.6 us -> 86.7 us
    ppermute x8 -> x5, waiting for transfers between devices: 21.6 us -> 31.6 us  [from_behind(): return lax.ppermute(block, axis, route)]
    ppermute x8 -> x5, starting transfers between devices: 14.9 us -> 9.15 us  [from_behind(): return lax.ppermute(block, axis, route)]
  transfers between devices with their start and end apart: 50 -> 47, of which waited for: 37 -> 34; matrix products, arithmetic and copies ran while one was open for 5% -> 4% of each run, Pallas kernels for 3% -> 3%
where the time goes in v1:
time: 336 us; the launch traced here: 329 us
  waiting for transfers between devices  169 us (50%)
  starting transfers between devices  86.7 us (26%)
  matrix products  39.2 us (12%)
  Pallas kernels  21.7 us (6%)
  other arithmetic  7.07 us (2%)
  local copies, waits for them, and re-layouts  4.65 us (1%)
    ppermute x18, waiting for transfers between devices, total(): got = [lax.ppermute(block, 'col', route(d)) for d in (2, 1, 3)]  46.7 us
    all_to_all x1, waiting for transfers between devices, update_block(): lax.all_to_all(sent, 'col', 0, 0, axis_index_groups=Z_GROUPS, tiled=True)  33.7 us
    ppermute x5, waiting for transfers between devices, from_behind(): return lax.ppermute(block, axis, route)  31.6 us
    ppermute x18, starting transfers between devices, total(): got = [lax.ppermute(block, 'col', route(d)) for d in (2, 1, 3)]  27.9 us
    pallas_call x3, Pallas kernels, inverse_factor(): pl.pallas_call(inverse_factor_kernel, grid=(1,), in_specs=[pl.BlockSpec((...  15 us
    ppermute x1, waiting for transfers between devices, update_block(): two = lax.ppermute(inner, 'col', along_x(2))  15 us
    ppermute x4, waiting for transfers between devices, with_mate(): other = lax.ppermute(half, 'col', MATE)  12.4 us
    ppermute x4, waiting for transfers between devices, update_block(): slices = [lax.ppermute(slices[d], both, across(-1, d)) for d in range(NX)]  12.3 us
  transfers between devices with their start and end apart: 47, of which 34 were waited for; matrix products, arithmetic and copies ran while one was open for 4% of the time, Pallas kernels for 3%

profile of v1, /device:TPU:16, one launch (start us, length us, event | category | flops | bytes accessed | tf_op | source)
XLA Modules:
  0.0 329.5 jit_solution(6261792859558906041)
XLA Ops:
  1.9 3.1 collective-permute-start.1
  9.1 1.6 collective-permute-start.2
  11.2 9.2 %collective-permute-done.5.refs_7_ = bf16[512,128]{1,0:T(8,128)(2,1)S(1)} collective-permute-done((bf16[512,128]{1,0:T(8,128)(2,1)S(1)}, bf16[512,128]{1,0:T(8,128)(2,1)S(1)}, u32[]{:S(2)}, u32[]{:S(2)}) %collective-permute-start.5) | collective-permute-done | bytes 131104 | tf_op jit(solution)/shard_map/ppermute | solution.py:165
  20.4 3.1 collective-permute-done.3.refs_5_
  23.5 2.4 collective-permute-start.7
  26.0 2.6 collective-permute-start.8
  28.6 15.0 %collective-permute-done.8.refs_10_ = bf16[256,128]{1,0:T(8,128)(2,1)S(1)} collective-permute-done((bf16[256,128]{1,0:T(8,128)(2,1)S(1)}, bf16[256,128]{1,0:T(8,128)(2,1)S(1)}, u32[]{:S(2)}, u32[]{:S(2)}) %collective-permute-start.8) | collective-permute-done | bytes 65568 | tf_op jit(solution)/shard_map/ppermute | solution.py:171
  44.5 6.6 %shard_map.95 = f32[8,272,512]{2,1,0:T(8,128)S(1)} custom-call(bf16[2304,128]{1,0:T(8,128)(2,1)S(1)} %pad_maximum_fusion.refs_0_.refs_8_, bf16[2304,128]{1,0:T(8,128)(2,1)S(1)} %collective-permute-done.6.refs_1_.refs_9_, bf16[2048,128]{1,0:T(8,128)(2,1)S(1)} %collective-permute-done.1.refs_2_, bf16[2304,128]{1,0:T(8,128)(2,1)S(1)} %collective-permute-done.7.refs_3_.refs_11_, ...), custom_call_target="tpu_custom_call" | custom-call | flops 2147483648 | bytes 8388608 | tf_op jit(solution)/shard_map/pallas_call | solution.py:139
  51.2 1.9 convert_element_type.59
  53.1 8.6 %all-to-all-start = ((f16[8,272,512]{2,1,0:T(8,128)(2,1)}), f16[8,272,512]{2,1,0:T(8,128)(2,1)S(1)}, u32[]{:S(2)}, u32[]{:S(2)}) async-start(f16[8,272,512]{2,1,0:T(8,128)(2,1)} %convert_element_type.59), calls=%async_computation | async-start | bytes 4456448 | tf_op jit(solution)/shard_map/all_to_all | solution.py:173
  61.7 2.1 collective-permute-start.9
  63.9 8.5 %collective-permute-done.9 = bf16[2048,128]{1,0:T(8,128)(2,1)} collective-permute-done((bf16[2048,128]{1,0:T(8,128)(2,1)S(1)}, bf16[2048,128]{1,0:T(8,128)(2,1)}, u32[]{:S(2)}, u32[]{:S(2)}) %collective-permute-start.9) | collective-permute-done | bytes 524320 | tf_op jit(solution)/shard_map/ppermute | solution.py:39
  72.3 9.7 %fusion.13 = f32[2048,384]{1,0:T(8,128)} fusion(bf16[2048,2048]{1,0:T(8,128)(2,1)} %param.14, bf16[2048,128]{1,0:T(8,128)(2,1)} %collective-permute-done.9, bf16[2048,128]{1,0:T(8,128)(2,1)S(1)} %copy-done.12, bf16[2048,128]{1,0:T(8,128)(2,1)} %param.15), kind=kOutput, calls=%fused_computation.16 | convolution fusion | flops 3225944064 | bytes 13107200 | tf_op jit(solution)/shard_map/dot_general | solution.py:228
  82.1 33.7 %all-to-all-done = f16[8,272,512]{2,1,0:T(8,128)(2,1)S(1)} async-done(((f16[8,272,512]{2,1,0:T(8,128)(2,1)}), f16[8,272,512]{2,1,0:T(8,128)(2,1)S(1)}, u32[]{:S(2)}, u32[]{:S(2)}) %all-to-all-start) | async-done | bytes 2228256 | tf_op jit(solution)/shard_map/all_to_all | solution.py:173
  118.4 4.4 %collective-permute-done.10 = f32[256,128]{1,0:T(8,128)S(1)} collective-permute-done((f32[256,128]{1,0:T(8,128)S(1)}, f32[256,128]{1,0:T(8,128)S(1)}, u32[]{:S(2)}, u32[]{:S(2)}) %collective-permute-start.10) | collective-permute-done | bytes 131104 | tf_op jit(solution)/shard_map/ppermute | solution.py:191
  123.8 2.1 collective-permute-start.12
  127.1 5.6 %collective-permute-done.13 = f32[256,128]{1,0:T(8,128)S(1)} collective-permute-done((f32[256,128]{1,0:T(8,128)S(1)}, f32[256,128]{1,0:T(8,128)S(1)}, u32[]{:S(2)}, u32[]{:S(2)}) %collective-permute-start.13) | collective-permute-done | bytes 131104 | tf_op jit(solution)/shard_map/ppermute | solution.py:43
  132.7 2.6 collective-permute-done.12
  135.3 4.2 %collective-permute-start.14 = (f32[256,128]{1,0:T(8,128)S(1)}, f32[256,128]{1,0:T(8,128)S(1)}, u32[]{:S(2)}, u32[]{:S(2)}) collective-permute-start(f32[256,128]{1,0:T(8,128)S(1)} %add_add_fusion.6), channel_id=1, source_target_pairs={{0,1},{1,0},{2,3},{3,2},{4,5},{5,4},{6,7},{7,6},{8,9},{9,8},{10,11... | collective-permute-start | bytes 393224 | tf_op jit(solution)/shard_map/ppermute | solution.py:180
  139.5 2.9 collective-permute-done.14
  143.8 3.2 collective-permute-start.17
  147.2 4.3 %collective-permute-done.16 = f32[384,128]{1,0:T(8,128)S(1)} collective-permute-done((f32[384,128]{1,0:T(8,128)S(1)}, f32[384,128]{1,0:T(8,128)S(1)}, u32[]{:S(2)}, u32[]{:S(2)}) %collective-permute-start.16) | collective-permute-done | bytes 196640 | tf_op jit(solution)/shard_map/ppermute | solution.py:43
  152.3 2.1 collective-permute-done.15
  155.4 2.1 collective-permute-start.18
  157.6 5.0 %shard_map.96 = f32[128,128]{1,0:T(8,128)} custom-call(f32[384,128]{1,0:T(8,128)} %copy-done.7), custom_call_target="tpu_custom_call" | custom-call | flops 40000000 | bytes 131072 | tf_op jit(solution)/shard_map/pallas_call | solution.py:83
  162.6 2.0 collective-permute-start.21
  165.6 2.6 collective-permute-start.19
  168.2 4.3 %collective-permute-done.21 = f32[256,128]{1,0:T(8,128)S(1)} collective-permute-done((f32[256,128]{1,0:T(8,128)S(1)}, f32[256,128]{1,0:T(8,128)S(1)}, u32[]{:S(2)}, u32[]{:S(2)}) %collective-permute-start.21) | collective-permute-done | bytes 131104 | tf_op jit(solution)/shard_map/ppermute | solution.py:43
  172.5 1.6 collective-permute-done.20
  174.1 4.6 %collective-permute-done.19 = f32[256,128]{1,0:T(8,128)S(1)} collective-permute-done((f32[256,128]{1,0:T(8,128)S(1)}, f32[256,128]{1,0:T(8,128)S(1)}, u32[]{:S(2)}, u32[]{:S(2)}) %collective-permute-start.19) | collective-permute-done | bytes 131104 | tf_op jit(solution)/shard_map/ppermute | solution.py:43
  178.9 5.0 %collective-permute-done.22 = f32[256,128]{1,0:T(8,128)S(1)} collective-permute-done((f32[256,128]{1,0:T(8,128)S(1)}, f32[256,128]{1,0:T(8,128)S(1)}, u32[]{:S(2)}, u32[]{:S(2)}) %collective-permute-start.22) | collective-permute-done | bytes 131104 | tf_op jit(solution)/shard_map/ppermute | solution.py:180
  186.4 3.2 collective-permute-start.25
  189.6 3.6 %collective-permute-done.24 = f32[384,128]{1,0:T(8,128)S(1)} collective-permute-done((f32[384,128]{1,0:T(8,128)S(1)}, f32[384,128]{1,0:T(8,128)S(1)}, u32[]{:S(2)}, u32[]{:S(2)}) %collective-permute-start.24) | collective-permute-done | bytes 196640 | tf_op jit(solution)/shard_map/ppermute | solution.py:43
  193.3 1.7 collective-permute-done.25
  194.9 1.9 collective-permute-done.23
  198.4 5.0 %shard_map.97 = f32[128,128]{1,0:T(8,128)} custom-call(f32[384,128]{1,0:T(8,128)} %copy-done.8), custom_call_target="tpu_custom_call" | custom-call | flops 40000000 | bytes 131072 | tf_op jit(solution)/shard_map/pallas_call | solution.py:83
  205.9 1.6 collective-permute-start.28
  207.5 3.8 %collective-permute-start.27 = (f32[256,128]{1,0:T(8,128)S(1)}, f32[256,128]{1,0:T(8,128)S(1)}, u32[]{:S(2)}, u32[]{:S(2)}) collective-permute-start(f32[256,128]{1,0:T(8,128)S(1)} %select_add_fusion), channel_id=1, source_target_pairs={{0,4},{1,5},{2,6},{3,7},{4,0},{5,1},{6,2},{7,3},{8,12},{9,13},{10,... | collective-permute-start | bytes 393224 | tf_op jit(solution)/shard_map/ppermute | solution.py:43
  211.3 2.3 collective-permute-done.29
  214.3 4.4 %collective-permute-done.27 = f32[256,128]{1,0:T(8,128)S(1)} collective-permute-done((f32[256,128]{1,0:T(8,128)S(1)}, f32[256,128]{1,0:T(8,128)S(1)}, u32[]{:S(2)}, u32[]{:S(2)}) %collective-permute-start.27) | collective-permute-done | bytes 131104 | tf_op jit(solution)/shard_map/ppermute | solution.py:43
  219.3 4.5 %collective-permute-done.30 = f32[256,128]{1,0:T(8,128)S(1)} collective-permute-done((f32[256,128]{1,0:T(8,128)S(1)}, f32[256,128]{1,0:T(8,128)S(1)}, u32[]{:S(2)}, u32[]{:S(2)}) %collective-permute-start.30) | collective-permute-done | bytes 131104 | tf_op jit(solution)/shard_map/ppermute | solution.py:180
  226.6 3.0 collective-permute-start.33
  230.7 2.5 collective-permute-done.32
  233.2 1.7 collective-permute-done.33
  234.9 2.0 collective-permute-done.31
  237.6 5.0 %shard_map.98 = f32[128,128]{1,0:T(8,128)} custom-call(f32[384,128]{1,0:T(8,128)} %copy-done.9), custom_call_target="tpu_custom_call" | custom-call | flops 40000000 | bytes 131072 | tf_op jit(solution)/shard_map/pallas_call | solution.py:83
  244.3 1.9 collective-permute-start.41
  246.3 1.9 collective-permute-start.40
  248.2 2.6 collective-permute-start.39
  250.8 2.0 collective-permute-start.38
  254.1 4.2 %collective-permute-start.37 = (bf16[512,128]{1,0:T(8,128)(2,1)S(1)}, bf16[512,128]{1,0:T(8,128)(2,1)S(1)}, u32[]{:S(2)}, u32[]{:S(2)}) collective-permute-start(bf16[512,128]{1,0:T(8,128)(2,1)S(1)} %convolution_convert_fusion), channel_id=1, source_target_pairs={{0,2},{1,3},{2,4},{3,5},{4,6},{5,7},{6,0},{7,1},{8,10},{9,11},{10,... | collective-permute-start | bytes 393224 | tf_op jit(solution)/shard_map/ppermute | solution.py:237
  259.4 4.7 %collective-permute-start.36 = (bf16[512,128]{1,0:T(8,128)(2,1)S(1)}, bf16[512,128]{1,0:T(8,128)(2,1)S(1)}, u32[]{:S(2)}, u32[]{:S(2)}) collective-permute-start(bf16[512,128]{1,0:T(8,128)(2,1)S(1)} %convolution_convert_fusion), channel_id=1, source_target_pairs={{0,4},{1,5},{2,6},{3,7},{4,0},{5,1},{6,2},{7,3},{8,12},{9,13},{10,... | collective-permute-start | bytes 393224 | tf_op jit(solution)/shard_map/ppermute | solution.py:237
  264.1 2.4 collective-permute-start.35
  266.8 9.3 %collective-permute-done.35 = bf16[512,128]{1,0:T(8,128)(2,1)S(1)} collective-permute-done((bf16[512,128]{1,0:T(8,128)(2,1)S(1)}, bf16[512,128]{1,0:T(8,128)(2,1)S(1)}, u32[]{:S(2)}, u32[]{:S(2)}) %collective-permute-start.35) | collective-permute-done | bytes 131104 | tf_op jit(solution)/shard_map/ppermute | solution.py:237
  276.3 6.0 %convolution_bitcast_fusion = f32[2048,256]{1,0:T(8,128)S(1)} fusion(bf16[2048,2048]{1,0:T(8,128)(2,1)} %param.14, bf16[2048,128]{1,0:T(8,128)(2,1)S(1)} %constant_dynamic-slice_fusion, bf16[2048,128]{1,0:T(8,128)(2,1)S(1)} %constant_dynamic-slice_fusion.1), kind=kOutput, calls=%fused_computation.8 | convolution fusion | flops 2149580800 | bytes 11534336 | tf_op jit(solution)/shard_map/dot_general | solution.py:238
  282.7 3.7 %fusion.1 = f32[256,384]{1,0:T(8,128)S(1)} fusion(f32[2048,128]{1,0:T(8,128)S(1)} %get-tuple-element.70, f32[2048,128]{1,0:T(8,128)S(1)} %get-tuple-element.45, f32[2048,128]{1,0:T(8,128)S(1)} %get-tuple-element.46, f32[2048,128]{1,0:T(8,128)S(1)} %get-tuple-element.71, f32[2048,128]{1,0:T(8,128)S(1)} %get-tuple-element.44), kind=kOutput, calls=%fused_computation.2 | convolution fusion | flops 2418016256 | bytes 5636096 | tf_op jit(solution)/shard_map/dot_general | solution.py:242
  286.5 1.9 collective-permute-start.43
  288.5 1.9 collective-permute-start.42
  290.4 8.1 %collective-permute-done.43 = bf16[256,512]{1,0:T(8,128)(2,1)S(1)} collective-permute-done((bf16[256,512]{1,0:T(8,128)(2,1)S(1)}, bf16[256,512]{1,0:T(8,128)(2,1)S(1)}, u32[]{:S(2)}, u32[]{:S(2)}) %collective-permute-start.43) | collective-permute-done | bytes 262176 | tf_op jit(solution)/shard_map/ppermute | solution.py:39
  298.4 2.1 collective-permute-done.42
  306.9 1.9 collective-permute-start.44
  308.8 6.3 %collective-permute-done.44 = bf16[256,512]{0,1:T(8,128)(2,1)S(1)} collective-permute-done((bf16[256,512]{0,1:T(8,128)(2,1)S(1)}, bf16[256,512]{0,1:T(8,128)(2,1)S(1)}, u32[]{:S(2)}, u32[]{:S(2)}) %collective-permute-start.44) | collective-permute-done | bytes 262176 | tf_op jit(solution)/shard_map/ppermute | solution.py:39
  318.4 6.7 %collective-permute-done.45 = f32[256,128]{1,0:T(8,128)S(1)} collective-permute-done((f32[256,128]{1,0:T(8,128)S(1)}, f32[256,128]{1,0:T(8,128)S(1)}, u32[]{:S(2)}, u32[]{:S(2)}) %collective-permute-start.45) | collective-permute-done | bytes 131104 | tf_op jit(solution)/shard_map/ppermute | solution.py:39
  325.4 2.8 convolution_subtract_fusion
  (140 shorter events, 44.2 us)
Async XLA Ops:
  0.6 10.1 %copy-start.5 = (bf16[2048,128]{1,0:T(8,128)(2,1)S(1)}, bf16[2048,128]{1,0:T(8,128)(2,1)}, u32[]{:S(2)}) copy-start(bf16[2048,128]{1,0:T(8,128)(2,1)} %param.9) | copy-start | bytes 1572868
  0.6 10.5 %copy-start.6 = (bf16[2048,128]{1,0:T(8,128)(2,1)S(1)}, bf16[2048,128]{1,0:T(8,128)(2,1)}, u32[]{:S(2)}) copy-start(bf16[2048,128]{1,0:T(8,128)(2,1)} %param.8) | copy-start | bytes 1572868
  1.9 7.3 %collective-permute-start = (bf16[2048,128]{1,0:T(8,128)(2,1)S(1)}, bf16[2048,128]{1,0:T(8,128)(2,1)S(1)}, u32[]{:S(2)}, u32[]{:S(2)}) collective-permute-start(bf16[2048,128]{1,0:T(8,128)(2,1)S(1)} %broadcast_select_fusion.1), channel_id=1, source_target_pairs={{0,224},{1,225},{2,226},{3,227},{4,228},{5,229},{6,230},{7,231},{8... | collective-permute-start | bytes 1572872 | tf_op jit(solution)/shard_map/ppermute | solution.py:161
  1.9 21.7 %collective-permute-start.1 = (bf16[2048,128]{1,0:T(8,128)(2,1)}, bf16[2048,128]{1,0:T(8,128)(2,1)S(1)}, u32[]{:S(2)}, u32[]{:S(2)}) collective-permute-start(bf16[2048,128]{1,0:T(8,128)(2,1)} %param.8), channel_id=1, source_target_pairs={{0,16},{1,17},{2,18},{3,19},{4,20},{5,21},{6,22},{7,23},{8,24},{9,... | collective-permute-start | bytes 1572872 | tf_op jit(solution)/shard_map/ppermute | solution.py:162
  6.2 14.2 %collective-permute-start.5 = (bf16[512,128]{1,0:T(8,128)(2,1)S(1)}, bf16[512,128]{1,0:T(8,128)(2,1)S(1)}, u32[]{:S(2)}, u32[]{:S(2)}) collective-permute-start(bf16[512,128]{1,0:T(8,128)(2,1)S(1)} %get-tuple-element.49), channel_id=1, source_target_pairs={{0,248},{1,249},{2,250},{3,251},{4,252},{5,253},{6,254},{7,255},{8... | collective-permute-start | bytes 393224 | tf_op jit(solution)/shard_map/ppermute | solution.py:165
  7.0 13.4 %collective-permute-start.4 = (bf16[512,128]{1,0:T(8,128)(2,1)S(1)}, bf16[512,128]{1,0:T(8,128)(2,1)S(1)}, u32[]{:S(2)}, u32[]{:S(2)}) collective-permute-start(bf16[512,128]{1,0:T(8,128)(2,1)S(1)} %get-tuple-element.50), channel_id=1, source_target_pairs={{0,240},{1,241},{2,242},{3,243},{4,244},{5,245},{6,246},{7,247},{8... | collective-permute-start | bytes 393224 | tf_op jit(solution)/shard_map/ppermute | solution.py:165
  8.5 15.0 %collective-permute-start.3 = (bf16[512,128]{1,0:T(8,128)(2,1)S(1)}, bf16[512,128]{1,0:T(8,128)(2,1)S(1)}, u32[]{:S(2)}, u32[]{:S(2)}) collective-permute-start(bf16[512,128]{1,0:T(8,128)(2,1)S(1)} %get-tuple-element.51), channel_id=1, source_target_pairs={{0,232},{1,233},{2,234},{3,235},{4,236},{5,237},{6,238},{7,239},{8... | collective-permute-start | bytes 393224 | tf_op jit(solution)/shard_map/ppermute | solution.py:165
  9.1 14.4 %collective-permute-start.2 = (bf16[512,128]{1,0:T(8,128)(2,1)S(1)}, bf16[512,128]{1,0:T(8,128)(2,1)S(1)}, u32[]{:S(2)}, u32[]{:S(2)}) collective-permute-start(bf16[512,128]{1,0:T(8,128)(2,1)S(1)} %get-tuple-element.52), channel_id=1, source_target_pairs={{0,224},{1,225},{2,226},{3,227},{4,228},{5,229},{6,230},{7,231},{8... | collective-permute-start | bytes 393224 | tf_op jit(solution)/shard_map/ppermute | solution.py:165
  23.5 20.0 %collective-permute-start.7 = (bf16[2304,128]{1,0:T(8,128)(2,1)S(1)}, bf16[2304,128]{1,0:T(8,128)(2,1)S(1)}, u32[]{:S(2)}, u32[]{:S(2)}) collective-permute-start(bf16[2304,128]{1,0:T(8,128)(2,1)S(1)} %pad_maximum_fusion.refs_0_.refs_8_), channel_id=1, source_target_pairs={{0,24},{1,25},{2,26},{3,27},{4,28},{5,29},{6,30},{7,31},{8,0},{9,1... | collective-permute-start | bytes 1769480 | tf_op jit(solution)/shard_map/ppermute | solution.py:170
  26.0 18.6 %collective-permute-start.6 = (bf16[2304,128]{1,0:T(8,128)(2,1)S(1)}, bf16[2304,128]{1,0:T(8,128)(2,1)S(1)}, u32[]{:S(2)}, u32[]{:S(2)}) collective-permute-start(bf16[2304,128]{1,0:T(8,128)(2,1)S(1)} %pad_maximum_fusion.refs_0_.refs_8_), channel_id=1, source_target_pairs={{0,8},{1,9},{2,10},{3,11},{4,12},{5,13},{6,14},{7,15},{8,16},{9,17... | collective-permute-start | bytes 1769480 | tf_op jit(solution)/shard_map/ppermute | solution.py:170
  26.0 17.6 %collective-permute-start.8 = (bf16[256,128]{1,0:T(8,128)(2,1)S(1)}, bf16[256,128]{1,0:T(8,128)(2,1)S(1)}, u32[]{:S(2)}, u32[]{:S(2)}) collective-permute-start(bf16[256,128]{1,0:T(8,128)(2,1)S(1)} %pad_maximum_fusion.9), channel_id=1, source_target_pairs={{0,16},{1,17},{2,18},{3,19},{4,20},{5,21},{6,22},{7,23},{8,24},{9,... | collective-permute-start | bytes 196616 | tf_op jit(solution)/shard_map/ppermute | solution.py:171
  53.1 8.6 %copy-start.13 = (bf16[2048,128]{1,0:T(8,128)(2,1)S(1)}, bf16[2048,128]{1,0:T(8,128)(2,1)}, u32[]{:S(2)}) copy-start(bf16[2048,128]{1,0:T(8,128)(2,1)} %param.12) | copy-start | bytes 1572868
  53.1 19.2 %copy-start.12 = (bf16[2048,128]{1,0:T(8,128)(2,1)S(1)}, bf16[2048,128]{1,0:T(8,128)(2,1)}, u32[]{:S(2)}) copy-start(bf16[2048,128]{1,0:T(8,128)(2,1)} %param.13) | copy-start | bytes 1572868
  53.1 62.6 %all-to-all-start = ((f16[8,272,512]{2,1,0:T(8,128)(2,1)}), f16[8,272,512]{2,1,0:T(8,128)(2,1)S(1)}, u32[]{:S(2)}, u32[]{:S(2)}) async-start(f16[8,272,512]{2,1,0:T(8,128)(2,1)} %convert_element_type.59), calls=%async_computation | async-start | bytes 4456448 | tf_op jit(solution)/shard_map/all_to_all | solution.py:173
  61.7 10.6 %collective-permute-start.9 = (bf16[2048,128]{1,0:T(8,128)(2,1)S(1)}, bf16[2048,128]{1,0:T(8,128)(2,1)}, u32[]{:S(2)}, u32[]{:S(2)}) collective-permute-start(bf16[2048,128]{1,0:T(8,128)(2,1)S(1)} %copy-done.13), channel_id=1, source_target_pairs={{0,32},{32,64},{64,96},{96,128},{128,160},{160,192},{192,224},{1,3... | collective-permute-start | bytes 1572872 | tf_op jit(solution)/shard_map/ppermute | solution.py:39
  117.8 5.1 %collective-permute-start.10 = (f32[256,128]{1,0:T(8,128)S(1)}, f32[256,128]{1,0:T(8,128)S(1)}, u32[]{:S(2)}, u32[]{:S(2)}) collective-permute-start(f32[256,128]{1,0:T(8,128)S(1)} %slice_select_fusion.2), channel_id=1, source_target_pairs={{0,1},{1,0},{2,3},{3,2},{4,5},{5,4},{6,7},{7,6},{8,9},{9,8},{10,11... | collective-permute-start | bytes 393224 | tf_op jit(solution)/shard_map/ppermute | solution.py:191
  122.9 9.8 %collective-permute-start.13 = (f32[256,128]{1,0:T(8,128)S(1)}, f32[256,128]{1,0:T(8,128)S(1)}, u32[]{:S(2)}, u32[]{:S(2)}) collective-permute-start(f32[256,128]{1,0:T(8,128)S(1)} %select_add_fusion.2), channel_id=1, source_target_pairs={{0,6},{1,7},{2,0},{3,1},{4,2},{5,3},{6,4},{7,5},{8,14},{9,15},{10,... | collective-permute-start | bytes 393224 | tf_op jit(solution)/shard_map/ppermute | solution.py:43
  123.8 11.5 %collective-permute-start.12 = (f32[256,128]{1,0:T(8,128)S(1)}, f32[256,128]{1,0:T(8,128)S(1)}, u32[]{:S(2)}, u32[]{:S(2)}) collective-permute-start(f32[256,128]{1,0:T(8,128)S(1)} %select_add_fusion.2), channel_id=1, source_target_pairs={{0,2},{1,3},{2,4},{3,5},{4,6},{5,7},{6,0},{7,1},{8,10},{9,11},{10,... | collective-permute-start | bytes 393224 | tf_op jit(solution)/shard_map/ppermute | solution.py:43
  125.9 9.4 %collective-permute-start.11 = (f32[256,128]{1,0:T(8,128)S(1)}, f32[256,128]{1,0:T(8,128)S(1)}, u32[]{:S(2)}, u32[]{:S(2)}) collective-permute-start(f32[256,128]{1,0:T(8,128)S(1)} %select_add_fusion.2), channel_id=1, source_target_pairs={{0,4},{1,5},{2,6},{3,7},{4,0},{5,1},{6,2},{7,3},{8,12},{9,13},{10,... | collective-permute-start | bytes 393224 | tf_op jit(solution)/shard_map/ppermute | solution.py:43
  135.3 7.1 %collective-permute-start.14 = (f32[256,128]{1,0:T(8,128)S(1)}, f32[256,128]{1,0:T(8,128)S(1)}, u32[]{:S(2)}, u32[]{:S(2)}) collective-permute-start(f32[256,128]{1,0:T(8,128)S(1)} %add_add_fusion.6), channel_id=1, source_target_pairs={{0,1},{1,0},{2,3},{3,2},{4,5},{5,4},{6,7},{7,6},{8,9},{9,8},{10,11... | collective-permute-start | bytes 393224 | tf_op jit(solution)/shard_map/ppermute | solution.py:180
  143.7 7.9 %collective-permute-start.16 = (f32[384,128]{1,0:T(8,128)S(1)}, f32[384,128]{1,0:T(8,128)S(1)}, u32[]{:S(2)}, u32[]{:S(2)}) collective-permute-start(f32[384,128]{1,0:T(8,128)S(1)} %pad_maximum_fusion.6), channel_id=1, source_target_pairs={{0,8},{1,9},{2,10},{3,11},{4,12},{5,13},{6,14},{7,15},{8,16},{9,17... | collective-permute-start | bytes 589832 | tf_op jit(solution)/shard_map/ppermute | solution.py:43
  143.8 8.5 %collective-permute-start.17 = (f32[384,128]{1,0:T(8,128)S(1)}, f32[384,128]{1,0:T(8,128)S(1)}, u32[]{:S(2)}, u32[]{:S(2)}) collective-permute-start(f32[384,128]{1,0:T(8,128)S(1)} %pad_maximum_fusion.6), channel_id=1, source_target_pairs={{0,24},{1,25},{2,26},{3,27},{4,28},{5,29},{6,30},{7,31},{8,0},{9,1... | collective-permute-start | bytes 589832 | tf_op jit(solution)/shard_map/ppermute | solution.py:43
  147.0 7.4 %collective-permute-start.15 = (f32[384,128]{1,0:T(8,128)S(1)}, f32[384,128]{1,0:T(8,128)S(1)}, u32[]{:S(2)}, u32[]{:S(2)}) collective-permute-start(f32[384,128]{1,0:T(8,128)S(1)} %pad_maximum_fusion.6), channel_id=1, source_target_pairs={{0,16},{1,17},{2,18},{3,19},{4,20},{5,21},{6,22},{7,23},{8,24},{9,... | collective-permute-start | bytes 589832 | tf_op jit(solution)/shard_map/ppermute | solution.py:43
  154.4 3.2 copy-start.7
  155.4 7.1 %collective-permute-start.18 = (f32[256,128]{1,0:T(8,128)S(1)}, f32[256,128]{1,0:T(8,128)S(1)}, u32[]{:S(2)}, u32[]{:S(2)}) collective-permute-start(f32[256,128]{1,0:T(8,128)S(1)} %slice_select_fusion.1), channel_id=1, source_target_pairs={{0,1},{1,0},{2,3},{3,2},{4,5},{5,4},{6,7},{7,6},{8,9},{9,8},{10,11... | collective-permute-start | bytes 393224 | tf_op jit(solution)/shard_map/ppermute | solution.py:191
  162.6 9.9 %collective-permute-start.21 = (f32[256,128]{1,0:T(8,128)S(1)}, f32[256,128]{1,0:T(8,128)S(1)}, u32[]{:S(2)}, u32[]{:S(2)}) collective-permute-start(f32[256,128]{1,0:T(8,128)S(1)} %select_add_fusion.1), channel_id=1, source_target_pairs={{0,6},{1,7},{2,0},{3,1},{4,2},{5,3},{6,4},{7,5},{8,14},{9,15},{10,... | collective-permute-start | bytes 393224 | tf_op jit(solution)/shard_map/ppermute | solution.py:43
  164.7 9.5 %collective-permute-start.20 = (f32[256,128]{1,0:T(8,128)S(1)}, f32[256,128]{1,0:T(8,128)S(1)}, u32[]{:S(2)}, u32[]{:S(2)}) collective-permute-start(f32[256,128]{1,0:T(8,128)S(1)} %select_add_fusion.1), channel_id=1, source_target_pairs={{0,2},{1,3},{2,4},{3,5},{4,6},{5,7},{6,0},{7,1},{8,10},{9,11},{10,... | collective-permute-start | bytes 393224 | tf_op jit(solution)/shard_map/ppermute | solution.py:43
  165.6 13.2 %collective-permute-start.19 = (f32[256,128]{1,0:T(8,128)S(1)}, f32[256,128]{1,0:T(8,128)S(1)}, u32[]{:S(2)}, u32[]{:S(2)}) collective-permute-start(f32[256,128]{1,0:T(8,128)S(1)} %select_add_fusion.1), channel_id=1, source_target_pairs={{0,4},{1,5},{2,6},{3,7},{4,0},{5,1},{6,2},{7,3},{8,12},{9,13},{10,... | collective-permute-start | bytes 393224 | tf_op jit(solution)/shard_map/ppermute | solution.py:43
  178.8 5.1 %collective-permute-start.22 = (f32[256,128]{1,0:T(8,128)S(1)}, f32[256,128]{1,0:T(8,128)S(1)}, u32[]{:S(2)}, u32[]{:S(2)}) collective-permute-start(f32[256,128]{1,0:T(8,128)S(1)} %add_add_fusion.5), channel_id=1, source_target_pairs={{0,1},{1,0},{2,3},{3,2},{4,5},{5,4},{6,7},{7,6},{8,9},{9,8},{10,11... | collective-permute-start | bytes 393224 | tf_op jit(solution)/shard_map/ppermute | solution.py:180
  186.3 7.0 %collective-permute-start.24 = (f32[384,128]{1,0:T(8,128)S(1)}, f32[384,128]{1,0:T(8,128)S(1)}, u32[]{:S(2)}, u32[]{:S(2)}) collective-permute-start(f32[384,128]{1,0:T(8,128)S(1)} %pad_maximum_fusion.7), channel_id=1, source_target_pairs={{0,8},{1,9},{2,10},{3,11},{4,12},{5,13},{6,14},{7,15},{8,16},{9,17... | collective-permute-start | bytes 589832 | tf_op jit(solution)/shard_map/ppermute | solution.py:43
  186.4 8.5 %collective-permute-start.25 = (f32[384,128]{1,0:T(8,128)S(1)}, f32[384,128]{1,0:T(8,128)S(1)}, u32[]{:S(2)}, u32[]{:S(2)}) collective-permute-start(f32[384,128]{1,0:T(8,128)S(1)} %pad_maximum_fusion.7), channel_id=1, source_target_pairs={{0,24},{1,25},{2,26},{3,27},{4,28},{5,29},{6,30},{7,31},{8,0},{9,1... | collective-permute-start | bytes 589832 | tf_op jit(solution)/shard_map/ppermute | solution.py:43
  189.6 7.2 %collective-permute-start.23 = (f32[384,128]{1,0:T(8,128)S(1)}, f32[384,128]{1,0:T(8,128)S(1)}, u32[]{:S(2)}, u32[]{:S(2)}) collective-permute-start(f32[384,128]{1,0:T(8,128)S(1)} %pad_maximum_fusion.7), channel_id=1, source_target_pairs={{0,16},{1,17},{2,18},{3,19},{4,20},{5,21},{6,22},{7,23},{8,24},{9,... | collective-permute-start | bytes 589832 | tf_op jit(solution)/shard_map/ppermute | solution.py:43
  196.8 1.6 copy-start.8
  197.9 6.5 %collective-permute-start.26 = (f32[256,128]{1,0:T(8,128)S(1)}, f32[256,128]{1,0:T(8,128)S(1)}, u32[]{:S(2)}, u32[]{:S(2)}) collective-permute-start(f32[256,128]{1,0:T(8,128)S(1)} %slice_select_fusion), channel_id=1, source_target_pairs={{0,1},{1,0},{2,3},{3,2},{4,5},{5,4},{6,7},{7,6},{8,9},{9,8},{10,11... | collective-permute-start | bytes 393224 | tf_op jit(solution)/shard_map/ppermute | solution.py:191
  204.5 9.1 %collective-permute-start.29 = (f32[256,128]{1,0:T(8,128)S(1)}, f32[256,128]{1,0:T(8,128)S(1)}, u32[]{:S(2)}, u32[]{:S(2)}) collective-permute-start(f32[256,128]{1,0:T(8,128)S(1)} %select_add_fusion), channel_id=1, source_target_pairs={{0,6},{1,7},{2,0},{3,1},{4,2},{5,3},{6,4},{7,5},{8,14},{9,15},{10,... | collective-permute-start | bytes 393224 | tf_op jit(solution)/shard_map/ppermute | solution.py:43
  205.9 8.4 %collective-permute-start.28 = (f32[256,128]{1,0:T(8,128)S(1)}, f32[256,128]{1,0:T(8,128)S(1)}, u32[]{:S(2)}, u32[]{:S(2)}) collective-permute-start(f32[256,128]{1,0:T(8,128)S(1)} %select_add_fusion), channel_id=1, source_target_pairs={{0,2},{1,3},{2,4},{3,5},{4,6},{5,7},{6,0},{7,1},{8,10},{9,11},{10,... | collective-permute-start | bytes 393224 | tf_op jit(solution)/shard_map/ppermute | solution.py:43
  207.5 11.3 %collective-permute-start.27 = (f32[256,128]{1,0:T(8,128)S(1)}, f32[256,128]{1,0:T(8,128)S(1)}, u32[]{:S(2)}, u32[]{:S(2)}) collective-permute-start(f32[256,128]{1,0:T(8,128)S(1)} %select_add_fusion), channel_id=1, source_target_pairs={{0,4},{1,5},{2,6},{3,7},{4,0},{5,1},{6,2},{7,3},{8,12},{9,13},{10,... | collective-permute-start | bytes 393224 | tf_op jit(solution)/shard_map/ppermute | solution.py:43
  218.8 5.1 %collective-permute-start.30 = (f32[256,128]{1,0:T(8,128)S(1)}, f32[256,128]{1,0:T(8,128)S(1)}, u32[]{:S(2)}, u32[]{:S(2)}) collective-permute-start(f32[256,128]{1,0:T(8,128)S(1)} %add_add_fusion.4), channel_id=1, source_target_pairs={{0,1},{1,0},{2,3},{3,2},{4,5},{5,4},{6,7},{7,6},{8,9},{9,8},{10,11... | collective-permute-start | bytes 393224 | tf_op jit(solution)/shard_map/ppermute | solution.py:180
  226.3 7.0 %collective-permute-start.32 = (f32[384,128]{1,0:T(8,128)S(1)}, f32[384,128]{1,0:T(8,128)S(1)}, u32[]{:S(2)}, u32[]{:S(2)}) collective-permute-start(f32[384,128]{1,0:T(8,128)S(1)} %pad_maximum_fusion.8), channel_id=1, source_target_pairs={{0,8},{1,9},{2,10},{3,11},{4,12},{5,13},{6,14},{7,15},{8,16},{9,17... | collective-permute-start | bytes 589832 | tf_op jit(solution)/shard_map/ppermute | solution.py:43
  226.6 8.4 %collective-permute-start.33 = (f32[384,128]{1,0:T(8,128)S(1)}, f32[384,128]{1,0:T(8,128)S(1)}, u32[]{:S(2)}, u32[]{:S(2)}) collective-permute-start(f32[384,128]{1,0:T(8,128)S(1)} %pad_maximum_fusion.8), channel_id=1, source_target_pairs={{0,24},{1,25},{2,26},{3,27},{4,28},{5,29},{6,30},{7,31},{8,0},{9,1... | collective-permute-start | bytes 589832 | tf_op jit(solution)/shard_map/ppermute | solution.py:43
  229.6 7.3 %collective-permute-start.31 = (f32[384,128]{1,0:T(8,128)S(1)}, f32[384,128]{1,0:T(8,128)S(1)}, u32[]{:S(2)}, u32[]{:S(2)}) collective-permute-start(f32[384,128]{1,0:T(8,128)S(1)} %pad_maximum_fusion.8), channel_id=1, source_target_pairs={{0,16},{1,17},{2,18},{3,19},{4,20},{5,21},{6,22},{7,23},{8,24},{9,... | collective-permute-start | bytes 589832 | tf_op jit(solution)/shard_map/ppermute | solution.py:43
  237.0 0.7 copy-start.9
  242.7 10.2 %collective-permute-start.34 = (f32[256,128]{1,0:T(8,128)S(1)}, f32[256,128]{1,0:T(8,128)S(1)}, u32[]{:S(2)}, u32[]{:S(2)}) collective-permute-start(f32[256,128]{1,0:T(8,128)S(1)} %slice.118), channel_id=1, source_target_pairs={{0,1},{1,0},{2,3},{3,2},{4,5},{5,4},{6,7},{7,6},{8,9},{9,8},{10,11... | collective-permute-start | bytes 393224 | tf_op jit(solution)/shard_map/ppermute | solution.py:180
  244.3 22.2 %collective-permute-start.41 = (bf16[512,128]{1,0:T(8,128)(2,1)S(1)}, bf16[512,128]{1,0:T(8,128)(2,1)S(1)}, u32[]{:S(2)}, u32[]{:S(2)}) collective-permute-start(bf16[512,128]{1,0:T(8,128)(2,1)S(1)} %fusion.19), channel_id=1, source_target_pairs={{0,32},{1,33},{2,34},{3,35},{4,36},{5,37},{6,38},{7,39},{8,40},{9,... | collective-permute-start | bytes 393224 | tf_op jit(solution)/shard_map/ppermute | solution.py:235
  246.3 20.3 %collective-permute-start.40 = (bf16[512,128]{1,0:T(8,128)(2,1)S(1)}, bf16[512,128]{1,0:T(8,128)(2,1)S(1)}, u32[]{:S(2)}, u32[]{:S(2)}) collective-permute-start(bf16[512,128]{1,0:T(8,128)(2,1)S(1)} %fusion.19), channel_id=1, source_target_pairs={{0,40},{1,41},{2,42},{3,43},{4,44},{5,45},{6,46},{7,47},{8,48},{9,... | collective-permute-start | bytes 393224 | tf_op jit(solution)/shard_map/ppermute | solution.py:235
  248.2 15.9 %collective-permute-start.39 = (bf16[512,128]{1,0:T(8,128)(2,1)S(1)}, bf16[512,128]{1,0:T(8,128)(2,1)S(1)}, u32[]{:S(2)}, u32[]{:S(2)}) collective-permute-start(bf16[512,128]{1,0:T(8,128)(2,1)S(1)} %fusion.19), channel_id=1, source_target_pairs={{0,48},{1,49},{2,50},{3,51},{4,52},{5,53},{6,54},{7,55},{8,56},{9,... | collective-permute-start | bytes 393224 | tf_op jit(solution)/shard_map/ppermute | solution.py:235
  250.8 8.6 %collective-permute-start.38 = (bf16[512,128]{1,0:T(8,128)(2,1)S(1)}, bf16[512,128]{1,0:T(8,128)(2,1)S(1)}, u32[]{:S(2)}, u32[]{:S(2)}) collective-permute-start(bf16[512,128]{1,0:T(8,128)(2,1)S(1)} %fusion.19), channel_id=1, source_target_pairs={{0,56},{1,57},{2,58},{3,59},{4,60},{5,61},{6,62},{7,63},{8,32},{9,... | collective-permute-start | bytes 393224 | tf_op jit(solution)/shard_map/ppermute | solution.py:235
  254.1 22.0 %collective-permute-start.37 = (bf16[512,128]{1,0:T(8,128)(2,1)S(1)}, bf16[512,128]{1,0:T(8,128)(2,1)S(1)}, u32[]{:S(2)}, u32[]{:S(2)}) collective-permute-start(bf16[512,128]{1,0:T(8,128)(2,1)S(1)} %convolution_convert_fusion), channel_id=1, source_target_pairs={{0,2},{1,3},{2,4},{3,5},{4,6},{5,7},{6,0},{7,1},{8,10},{9,11},{10,... | collective-permute-start | bytes 393224 | tf_op jit(solution)/shard_map/ppermute | solution.py:237
  259.4 16.7 %collective-permute-start.36 = (bf16[512,128]{1,0:T(8,128)(2,1)S(1)}, bf16[512,128]{1,0:T(8,128)(2,1)S(1)}, u32[]{:S(2)}, u32[]{:S(2)}) collective-permute-start(bf16[512,128]{1,0:T(8,128)(2,1)S(1)} %convolution_convert_fusion), channel_id=1, source_target_pairs={{0,4},{1,5},{2,6},{3,7},{4,0},{5,1},{6,2},{7,3},{8,12},{9,13},{10,... | collective-permute-start | bytes 393224 | tf_op jit(solution)/shard_map/ppermute | solution.py:237
  264.1 11.9 %collective-permute-start.35 = (bf16[512,128]{1,0:T(8,128)(2,1)S(1)}, bf16[512,128]{1,0:T(8,128)(2,1)S(1)}, u32[]{:S(2)}, u32[]{:S(2)}) collective-permute-start(bf16[512,128]{1,0:T(8,128)(2,1)S(1)} %convolution_convert_fusion), channel_id=1, source_target_pairs={{0,6},{1,7},{2,0},{3,1},{4,2},{5,3},{6,4},{7,5},{8,14},{9,15},{10,... | collective-permute-start | bytes 393224 | tf_op jit(solution)/shard_map/ppermute | solution.py:237
  276.3 6.0 %copy-start = (f32[2048,384]{1,0:T(8,128)S(1)}, f32[2048,384]{1,0:T(8,128)}, u32[]{:S(2)}) copy-start(f32[2048,384]{1,0:T(8,128)} %fusion.13) | copy-start | bytes 9437188
  282.7 3.7 %copy-start.1 = (f32[2048,128]{1,0:T(8,128)}, f32[2048,128]{1,0:T(8,128)S(1)}, u32[]{:S(2)}) copy-start(f32[2048,128]{1,0:T(8,128)S(1)} %get-tuple-element.45) | copy-start | bytes 3145732
  282.7 3.7 %copy-start.3 = (f32[2048,128]{1,0:T(8,128)}, f32[2048,128]{1,0:T(8,128)S(1)}, u32[]{:S(2)}) copy-start(f32[2048,128]{1,0:T(8,128)S(1)} %get-tuple-element.70) | copy-start | bytes 3145732
  286.5 11.9 %collective-permute-start.43 = (bf16[256,512]{1,0:T(8,128)(2,1)S(1)}, bf16[256,512]{1,0:T(8,128)(2,1)S(1)}, u32[]{:S(2)}, u32[]{:S(2)}) collective-permute-start(bf16[256,512]{1,0:T(8,128)(2,1)S(1)} %pad_maximum_fusion.2), channel_id=1, source_target_pairs={{0,64},{32,96},{64,128},{96,160},{128,192},{160,224},{1,65},{33,97... | collective-permute-start | bytes 786440 | tf_op jit(solution)/shard_map/ppermute | solution.py:39
  288.5 12.1 %collective-permute-start.42 = (bf16[256,512]{1,0:T(8,128)(2,1)S(1)}, bf16[256,512]{1,0:T(8,128)(2,1)S(1)}, u32[]{:S(2)}, u32[]{:S(2)}) collective-permute-start(bf16[256,512]{1,0:T(8,128)(2,1)S(1)} %pad_maximum_fusion.2), channel_id=1, source_target_pairs={{0,32},{32,64},{64,96},{96,128},{128,160},{160,192},{192,224},{1,3... | collective-permute-start | bytes 786440 | tf_op jit(solution)/shard_map/ppermute | solution.py:39
  298.4 2.1 copy-start.10
  300.5 1.0 copy-start.11
  304.7 20.8 %copy-start.2 = (f32[2048,128]{1,0:T(8,128)S(1)}, f32[2048,128]{1,0:T(8,128)}, u32[]{:S(2)}) copy-start(f32[2048,128]{1,0:T(8,128)} %copy-done.1) | copy-start | bytes 3145732
  304.7 20.8 %copy-start.4 = (f32[2048,128]{1,0:T(8,128)S(1)}, f32[2048,128]{1,0:T(8,128)}, u32[]{:S(2)}) copy-start(f32[2048,128]{1,0:T(8,128)} %copy-done.3) | copy-start | bytes 3145732
  306.9 8.3 %collective-permute-start.44 = (bf16[256,512]{0,1:T(8,128)(2,1)S(1)}, bf16[256,512]{0,1:T(8,128)(2,1)S(1)}, u32[]{:S(2)}, u32[]{:S(2)}) collective-permute-start(bf16[256,512]{0,1:T(8,128)(2,1)S(1)} %pad_maximum_fusion.3), channel_id=1, source_target_pairs={{0,64},{32,96},{64,128},{96,160},{128,192},{160,224},{1,65},{33,97... | collective-permute-start | bytes 786440 | tf_op jit(solution)/shard_map/ppermute | solution.py:39
  316.7 8.4 %collective-permute-start.45 = (f32[256,128]{1,0:T(8,128)S(1)}, f32[256,128]{1,0:T(8,128)S(1)}, u32[]{:S(2)}, u32[]{:S(2)}) collective-permute-start(f32[256,128]{1,0:T(8,128)S(1)} %convolution_add_fusion.2), channel_id=1, source_target_pairs={{0,128},{32,160},{64,192},{96,224},{1,129},{33,161},{65,193},{97,2... | collective-permute-start | bytes 393224 | tf_op jit(solution)/shard_map/ppermute | solution.py:39
